TPU v7x, 128 devices: a whole 4x4x4 slice. The times are simulated.
128 devices in a mesh: lon: 16 (over x, y_hi, core), lat: 8 (over z, y_lo).
Axes of the slice: x: 4, y: 4 (y_hi: 2, y_lo: 2; y = y_hi * 2 + y_lo), z: 4, core: 2. Of those that a mesh axis runs over, the one named last changes fastest.
Arguments:
- features: bfloat16 [128, 64, 4096], P(None, 'lat', 'lon'), may hold values from -45 to 45
- coarse_blocks: bfloat16 [16, 128, 40, 256], P('lon', 'lat'), may hold values from -6 to 6
- send_table: int32 [16, 8, 8, 8], P('lon'), may hold values from -1 to 15, as said below
- interp_src: int32 [2, 64, 4096], P(None, 'lat', 'lon'), may hold values from 0 to 16383, as said below
- interp_wt: float32 [2, 64, 4096], P(None, 'lat', 'lon'), may hold values from 0.25 to 1
- weight_in: bfloat16 [9, 128, 168], replicated, may hold values from -0.15625 to 0.15625
- weight_mid: bfloat16 [9, 128, 128], replicated, may hold values from -0.1875 to 0.1875
- weight_out: bfloat16 [9, 128, 128], replicated, may hold values from -0.1875 to 0.1875
- gain_in: float32 [128], replicated, may hold values from 0.5 to 2
- bias_in: float32 [128], replicated, may hold values from -3 to 3
- gain_mid: float32 [128], replicated, may hold values from 0.5 to 2
- bias_mid: float32 [128], replicated, may hold values from -3 to 3
- cotangent: bfloat16 [128, 64, 4096], P(None, 'lat', 'lon'), may hold values from -6 to 6
Outputs:
- output_field: bfloat16 [128, 64, 4096], P(None, 'lat', 'lon')
- grad_features: bfloat16 [128, 64, 4096], P(None, 'lat', 'lon')
- grad_weight_in: float32 [9, 128, 168], replicated
- grad_weight_mid: float32 [9, 128, 128], replicated
- grad_weight_out: float32 [9, 128, 128], replicated
Inputs may be any that keep to these rules, and one draw needn't show every extreme that they name: `send_table`: for column j, owner row o and destination row i the used slots come first and hold distinct block indices, the rest are -1; rows more than half of 8 apart exchange nothing, and an owner always fills all 8 slots for its own row. `interp_src`: every index points at a used slot of the cell's own pool.
All inputs are finite; a program needn't handle non-finite values.
Results may differ from a plain program's by a relative error of at most 0.014.
Values may be sent and summed in bfloat16 or wider, within the bound.
A program may use at most 64 MiB of HBM per device.

v0:
```python
import math

import jax
import jax.numpy as jnp
from jax import lax
from jax.sharding import PartitionSpec as P

G = 32


def with_halo(cells, sides, width, closed):
    for axis, dim in sides:
        count = lax.axis_size(axis)
        ends = count if closed else count - 1
        head = lax.slice_in_dim(cells, 0, width, axis=dim)
        tail = lax.slice_in_dim(cells, cells.shape[dim] - width, cells.shape[dim], axis=dim)
        cells = jnp.concatenate(
            [
                lax.ppermute(tail, axis, [(i, (i + 1) % count) for i in range(ends)]),
                cells,
                lax.ppermute(head, axis, [((i + 1) % count, i) for i in range(ends)]),
            ],
            axis=dim,
        )
    return cells


def pad_fine(field):
    beside_all = with_halo(field, (("lon", 2),), 1, True)
    return with_halo(beside_all, (("lat", 1),), 1, False)


def pad_coarse(field):
    beside_all = with_halo(field, (("lon", 2),), 1, True)
    return with_halo(beside_all, (("lat", 1),), 1, False)


def convolve(padded, weights, height, breadth):
    running = None
    for stencil in range(9):
        row_shift, col_shift = (stencil // 3, stencil % 3)
        window = padded[:, row_shift : row_shift + height, col_shift : col_shift + breadth].reshape(
            padded.shape[0], -1
        )
        partial_sum = jnp.dot(weights[stencil], window, preferred_element_type=jnp.float32)
        running = partial_sum if running is None else running + partial_sum
    return running.reshape(weights.shape[1], height, breadth)


def transposed(padded, weights, height, breadth):
    running = None
    for stencil in range(9):
        row_shift, col_shift = (2 - stencil // 3, 2 - stencil % 3)
        window = padded[:, row_shift : row_shift + height, col_shift : col_shift + breadth].reshape(
            padded.shape[0], -1
        )
        partial_sum = lax.dot_general(
            weights[stencil], window, (((0,), (0,)), ((), ())), preferred_element_type=jnp.float32
        )
        running = partial_sum if running is None else running + partial_sum
    return running.reshape(weights.shape[2], height, breadth)


def correlate(padded, gradient, height, breadth):
    flattened = gradient.reshape(gradient.shape[0], -1)
    stacked = []
    for stencil in range(9):
        row_shift, col_shift = (stencil // 3, stencil % 3)
        window = padded[:, row_shift : row_shift + height, col_shift : col_shift + breadth].reshape(
            padded.shape[0], -1
        )
        stacked.append(
            lax.dot_general(
                flattened, window, (((1,), (1,)), ((), ())), preferred_element_type=jnp.float32
            )
        )
    return jnp.stack(stacked)


def normalize(hidden, sums, squares, members, gain, bias):
    groups = sums.shape[0]
    average = sums / members
    variance = squares / members - average * average
    inv_scale = lax.rsqrt(variance + 1e-05)
    grouped = hidden.reshape(groups, -1)
    normed = ((grouped - average[:, None]) * inv_scale[:, None]).reshape(hidden.shape)
    affine = gain[:, None, None] * normed + bias[:, None, None]
    return (normed, affine, inv_scale)


def spread_stats(hidden, gain, bias, members):
    grouped = hidden.reshape(G, -1)
    sums, squares = lax.psum((jnp.sum(grouped, 1), jnp.sum(grouped * grouped, 1)), ("lon", "lat"))
    return normalize(hidden, sums, squares, members, gain, bias)


def spread_back(grad_act, affine, normed, inv_scale, gain, members):
    squash = jax.nn.sigmoid(affine)
    slope = grad_act * squash * (1.0 + affine * (1.0 - squash)) * gain[:, None, None]
    grouped = slope.reshape(G, -1)
    normed_group = normed.reshape(G, -1)
    sum_e, sum_en = lax.psum(
        (jnp.sum(grouped, 1), jnp.sum(grouped * normed_group, 1)), ("lon", "lat")
    )
    mean_e = sum_e / members
    mean_en = sum_en / members
    result = (grouped - mean_e[:, None] - normed_group * mean_en[:, None]) * inv_scale[:, None]
    return result.reshape(slope.shape).astype(jnp.bfloat16)


def pool_four(field):
    chans, height, breadth = field.shape
    return (
        field.astype(jnp.float32)
        .reshape(chans, height // 4, 4, breadth // 4, 4)
        .mean(axis=(2, 4))
        .astype(jnp.bfloat16)
    )


def up_four(field):
    return jnp.repeat(jnp.repeat(field, 4, axis=1), 4, axis=2)


def fold_four(field):
    chans, height, breadth = field.shape
    return field.reshape(chans, height // 4, 4, breadth // 4, 4).sum(axis=(2, 4))


def local(
    features,
    coarse_blocks,
    send_table,
    interp_src,
    interp_wt,
    weight_in,
    weight_mid,
    weight_out,
    gain_in,
    bias_in,
    gain_mid,
    bias_mid,
    cotangent,
):
    channels, height, breadth = features.shape
    lon_size = lax.axis_size("lon")
    lat_size = lax.axis_size("lat")
    my_row = lax.axis_index("lat")
    coarse_chans = coarse_blocks.shape[2]
    block_cells = coarse_blocks.shape[3]
    table = send_table[0]
    column = lax.all_gather(coarse_blocks, "lat", axis=1, tiled=True)
    column = column[0].reshape(lat_size, -1, coarse_chans, block_cells)
    wanted = lax.dynamic_index_in_dim(table, my_row, 1, keepdims=False)
    picked = column[jnp.arange(lat_size)[:, None], jnp.maximum(wanted, 0)]
    received = jnp.where((wanted >= 0)[:, :, None, None], picked, jnp.zeros((), jnp.bfloat16))
    gathered_pool = received.reshape(-1, coarse_chans, block_cells)
    values = gathered_pool[interp_src // block_cells, :, interp_src % block_cells]
    blended = jnp.sum(interp_wt[..., None] * values.astype(jnp.float32), 0)
    condition = jnp.transpose(blended, (2, 0, 1)).astype(jnp.bfloat16)
    inputs = jnp.concatenate([features, condition], axis=0)
    small_h, small_w = (height // 4, breadth // 4)
    members = channels // G * height * breadth * lon_size * lat_size
    factor = 1.0 / math.sqrt(height * breadth * lon_size * lat_size)
    pad_in = pad_fine(inputs)
    hidden_in = convolve(pad_in, weight_in, height, breadth)
    normed_in, affine_in, inv_in = spread_stats(hidden_in, gain_in, bias_in, members)
    act_in = jax.nn.silu(affine_in).astype(jnp.bfloat16)
    pooled = pool_four(act_in)
    pad_mid = pad_coarse(pooled)
    hidden_mid = convolve(pad_mid, weight_mid, small_h, small_w)
    normed_mid, affine_mid, inv_mid = spread_stats(hidden_mid, gain_mid, bias_mid, members // 16)
    act_mid = jax.nn.silu(affine_mid).astype(jnp.bfloat16)
    merged = (act_in.astype(jnp.float32) + up_four(act_mid).astype(jnp.float32)).astype(
        jnp.bfloat16
    )
    pad_out = pad_fine(merged)
    hidden_out = convolve(pad_out, weight_out, height, breadth)
    output_field = (features.astype(jnp.float32) + hidden_out).astype(jnp.bfloat16)
    pad_cot = pad_fine(cotangent)
    local_out = correlate(pad_out, cotangent, height, breadth)
    grad_weight_out = lax.psum(local_out, ("lon", "lat")) * factor
    grad_merged = transposed(pad_cot, weight_out, height, breadth)
    grad_small = fold_four(grad_merged)
    grad_mid_pre = spread_back(grad_small, affine_mid, normed_mid, inv_mid, gain_mid, members // 16)
    local_mid = correlate(pad_mid, grad_mid_pre, small_h, small_w)
    grad_weight_mid = lax.psum(local_mid, ("lon", "lat")) * factor
    grad_pooled = transposed(pad_coarse(grad_mid_pre), weight_mid, small_h, small_w)
    grad_act = grad_merged + up_four(grad_pooled) / 16.0
    grad_in_pre = spread_back(grad_act, affine_in, normed_in, inv_in, gain_in, members)
    local_in = correlate(pad_in, grad_in_pre, height, breadth)
    grad_weight_in = lax.psum(local_in, ("lon", "lat")) * factor
    grad_feat = transposed(pad_fine(grad_in_pre), weight_in[:, :, :channels], height, breadth)
    grad_features = (cotangent.astype(jnp.float32) + grad_feat).astype(jnp.bfloat16)
    return (output_field, grad_features, grad_weight_in, grad_weight_mid, grad_weight_out)


def solution(mesh):
    in_specs = (
        P(None, "lat", "lon"),
        P("lon", "lat", None, None),
        P("lon", None, None, None),
        P(None, "lat", "lon"),
        P(None, "lat", "lon"),
        P(),
        P(),
        P(),
        P(),
        P(),
        P(),
        P(),
        P(None, "lat", "lon"),
    )
    out_specs = (P(None, "lat", "lon"), P(None, "lat", "lon"), P(), P(), P())
    return jax.shard_map(local, mesh=mesh, in_specs=in_specs, out_specs=out_specs, check_vma=False)
```

profile of v0, /device:TPU:1, one launch (start us, length us, event | category | flops | bytes accessed | tf_op | source)
XLA Modules:
  0.0 740.6 jit_solution(77539884402225247)
XLA Ops:
  9.5 4.4 collective-permute-start.12
  15.2 3.2 collective-permute-done.13
  19.7 4.0 collective-permute-start.15
  25.0 2.1 collective-permute-done.15
  32.8 43.5 %all-gather.2.cloned.1.call-done = bf16[1,128,40,256]{3,2,0,1:T(8,128)(2,1)} async-done(((bf16[1,16,40,256]{3,2,0,1:T(8,128)(2,1)}), bf16[1,128,40,256]{3,2,0,1:T(8,128)(2,1)}) %all-gather.2.cloned.1.call-update) | async-done | bytes 2621456 | tf_op jit(solution)/shard_map/all_gather | solution.py:152
  76.3 2.4 gather_fusion
  80.0 4.6 copy.232
  84.6 47.9 %gather_fusion.1 = bf16[4096,40]{1,0:T(8,128)(2,1)S(1)} fusion(bf16[64,40,256]{1,2,0:T(8,128)(2,1)} %copy.232, s32[4096]{0:T(1024)S(1)} %bitcast.568), kind=kCustom, calls=%fused_computation.1 | custom fusion | bytes 688128 | tf_op jit(solution)/shard_map/gather | solution.py:158
  136.8 6.8 collective-permute-done
  143.6 4.0 collective-permute-done.1
  147.8 2.6 collective-permute-start.2
  152.9 3.7 collective-permute-done.3
  156.7 2.3 pad_maximum_fusion
  168.2 63.9 %all-reduce.3 = (f32[32]{0:T(128)S(1)}, f32[32]{0:T(128)S(1)}) all-reduce(f32[32]{0:T(128)S(1)} %reduce_sum.129, f32[32]{0:T(128)S(1)} %reduce_sum.126), channel_id=1, replica_groups=mesh['lon'=16,'lat'=8] {'lon','lat'}, use_global_device_ids=true, to_apply=%region_6.7 | all-reduce | flops 64 | bytes 512 | tf_op jit(solution)/shard_map/psum | solution.py:93
  232.9 2.2 collective-permute-start.4
  236.0 3.9 collective-permute-done.5
  243.7 2.7 collective-permute-done.7
  255.7 66.7 %all-reduce.2 = (f32[32]{0:T(128)}, f32[32]{0:T(128)}) all-reduce(f32[32]{0:T(128)} %reduce_sum.170, f32[32]{0:T(128)} %reduce_sum.136), channel_id=1, replica_groups=mesh['lon'=16,'lat'=8] {'lon','lat'}, use_global_device_ids=true, to_apply=%region_13.14 | all-reduce | flops 64 | bytes 512 | tf_op jit(solution)/shard_map/psum | solution.py:93
  326.8 63.8 %all-reduce.1 = (f32[32]{0:T(128)S(1)}, f32[32]{0:T(128)}) all-reduce(f32[32]{0:T(128)S(1)} %reduce_sum.178, f32[32]{0:T(128)S(1)} %reduce_sum.175), channel_id=1, replica_groups=mesh['lon'=16,'lat'=8] {'lon','lat'}, use_global_device_ids=true, to_apply=%region_20.21 | all-reduce | flops 64 | bytes 512 | tf_op jit(solution)/shard_map/psum | solution.py:102
  393.9 2.1 collective-permute-start.16
  403.0 4.0 collective-permute-start.19
  414.7 67.5 %all-reduce = (f32[32]{0:T(128)S(1)}, f32[32]{0:T(128)S(1)}) all-reduce(f32[32]{0:T(128)S(1)} %reduce_sum.184, f32[32]{0:T(128)S(1)} %reduce_sum.181), channel_id=1, replica_groups=mesh['lon'=16,'lat'=8] {'lon','lat'}, use_global_device_ids=true, to_apply=%region_26.27 | all-reduce | flops 64 | bytes 512 | tf_op jit(solution)/shard_map/psum | solution.py:102
  485.0 3.3 multiply_convert_fusion.1
  495.8 3.3 collective-permute-start.20
  501.4 3.6 collective-permute-start.10
  506.3 3.3 collective-permute-done.21
  511.7 4.8 collective-permute-start.23
  546.5 2.1 copy.269
  552.2 2.1 copy.273
  554.3 2.1 copy.274
  587.1 142.6 %all-reduce.7.cloned.1.call-done = (f32[9,128,168]{1,2,0:T(8,128)}, f32[9,128,128]{2,1,0:T(8,128)}, f32[9,128,128]{2,1,0:T(8,128)}) async-done(((f32[9,128,168]{1,2,0:T(8,128)}, f32[9,128,128]{2,1,0:T(8,128)}, f32[9,128,128]{2,1,0:T(8,128)}), (f32[9,128,168]{1,2,0:T(8,128)}, f32[9,128,128]{2,1,0:T(8,128)}, f32[9,128,128]{2,1,0:T(8,128)})) %all-reduce.7.cloned.1.call-update) | async-done | bytes 1953808 | tf_op jit(solution)/shard_map/psum | solution.py:192
  729.7 2.1 broadcast_multiply_fusion
  (390 shorter events, 147.1 us)
Async XLA Ops:
  7.2 69.1 %all-gather.2.cloned.1.call-start = ((), (), s32[]{:S(2)}) async-start(), calls=%async_computation | async-start | bytes 2949120 | tf_op jit(solution)/shard_map/all_gather | solution.py:152
  8.0 721.7 %all-reduce.7.cloned.1.call-start = ((), (), s32[]{:S(2)}) async-start(), calls=%async_computation.1 | async-start | bytes 3907584 | tf_op jit(solution)/shard_map/psum | solution.py:192
  9.5 5.7 collective-permute-start.12
  13.9 4.5 collective-permute-start.13
  18.4 6.6 collective-permute-start.14
  19.7 7.3 collective-permute-start.15
  84.6 47.9 %copy-start.51 = (f32[2,8,256]{2,1,0:T(8,128)S(1)}, f32[2,8,256]{2,1,0:T(8,128)}, u32[]{:S(2)}) copy-start(f32[2,8,256]{2,1,0:T(8,128)} %param.17) | copy-start | bytes 49156
  133.7 9.9 %collective-permute-start = (bf16[168,8,1]{2,0,1:T(8,128)(2,1)S(1)}, bf16[168,8,1]{2,0,1:T(8,128)(2,1)S(1)}, u32[]{:S(2)}, u32[]{:S(2)}) collective-permute-start(bf16[168,8,1]{2,0,1:T(8,128)(2,1)S(1)} %get-tuple-element.57), channel_id=1, source_target_pairs={{0,8},{8,16},{16,24},{24,32},{32,40},{40,48},{48,56},{56,64},{64,7... | collective-permute-start | bytes 8072 | tf_op jit(solution)/shard_map/ppermute | solution.py:19
  135.7 11.9 %collective-permute-start.1 = (bf16[168,8,1]{2,0,1:T(8,128)(2,1)S(1)}, bf16[168,8,1]{2,0,1:T(8,128)(2,1)S(1)}, u32[]{:S(2)}, u32[]{:S(2)}) collective-permute-start(bf16[168,8,1]{2,0,1:T(8,128)(2,1)S(1)} %get-tuple-element.58), channel_id=1, source_target_pairs={{8,0},{16,8},{24,16},{32,24},{40,32},{48,40},{56,48},{64,56},{72,6... | collective-permute-start | bytes 8072 | tf_op jit(solution)/shard_map/ppermute | solution.py:21
  147.8 5.2 collective-permute-start.2
  150.4 6.3 collective-permute-start.3
  166.5 66.0 %copy-start.59 = (f32[128]{0:T(128)S(1)}, f32[128]{0:T(128)}, u32[]{:S(2)}) copy-start(f32[128]{0:T(128)} %param.22) | copy-start | bytes 1540
  166.5 66.0 %copy-start.61 = (f32[128]{0:T(128)S(1)}, f32[128]{0:T(128)}, u32[]{:S(2)}) copy-start(f32[128]{0:T(128)} %param.21) | copy-start | bytes 1540
  232.9 3.0 collective-permute-start.4
  235.1 4.8 collective-permute-start.5
  239.9 3.8 collective-permute-start.6
  241.9 4.5 collective-permute-start.7
  323.3 69.5 %copy-start.57 = (f32[128]{0:T(128)}, f32[128]{0:T(128)S(1)}, u32[]{:S(2)}) copy-start(f32[128]{0:T(128)S(1)} %mul.340) | copy-start | bytes 1540
  323.5 69.3 %copy-start.58 = (f32[128]{0:T(128)}, f32[128]{0:T(128)S(1)}, u32[]{:S(2)}) copy-start(f32[128]{0:T(128)S(1)} %sub.155) | copy-start | bytes 1540
  393.9 7.8 %collective-permute-start.16 = (bf16[128,2,1]{0,2,1:T(2,128)(2,1)S(1)}, bf16[128,2,1]{0,2,1:T(2,128)(2,1)S(1)}, u32[]{:S(2)}, u32[]{:S(2)}) collective-permute-start(bf16[128,2,1]{0,2,1:T(2,128)(2,1)S(1)} %get-tuple-element.105), channel_id=1, source_target_pairs={{0,8},{8,16},{16,24},{24,32},{32,40},{40,48},{48,56},{56,64},{64,7... | collective-permute-start | bytes 1544 | tf_op jit(solution)/shard_map/ppermute | solution.py:19
  395.9 5.7 collective-permute-start.17
  401.7 5.3 collective-permute-start.18
  403.0 4.9 collective-permute-start.19
  488.5 11.6 %collective-permute-start.8 = (bf16[128,8,1]{2,0,1:T(8,128)(2,1)S(1)}, bf16[128,8,1]{2,0,1:T(8,128)(2,1)S(1)}, u32[]{:S(2)}, u32[]{:S(2)}) collective-permute-start(bf16[128,8,1]{2,0,1:T(8,128)(2,1)S(1)} %get-tuple-element.79), channel_id=1, source_target_pairs={{0,8},{8,16},{16,24},{24,32},{32,40},{40,48},{48,56},{56,64},{64,7... | collective-permute-start | bytes 6152 | tf_op jit(solution)/shard_map/ppermute | solution.py:19
  490.5 10.1 %collective-permute-start.9 = (bf16[128,8,1]{2,0,1:T(8,128)(2,1)S(1)}, bf16[128,8,1]{2,0,1:T(8,128)(2,1)S(1)}, u32[]{:S(2)}, u32[]{:S(2)}) collective-permute-start(bf16[128,8,1]{2,0,1:T(8,128)(2,1)S(1)} %get-tuple-element.80), channel_id=1, source_target_pairs={{8,0},{16,8},{24,16},{32,24},{40,32},{48,40},{56,48},{64,56},{72,6... | collective-permute-start | bytes 6152 | tf_op jit(solution)/shard_map/ppermute | solution.py:21
  495.8 10.5 %collective-permute-start.20 = (bf16[128,8,1]{2,0,1:T(8,128)(2,1)S(1)}, bf16[128,8,1]{2,0,1:T(8,128)(2,1)S(1)}, u32[]{:S(2)}, u32[]{:S(2)}) collective-permute-start(bf16[128,8,1]{2,0,1:T(8,128)(2,1)S(1)} %get-tuple-element.71), channel_id=1, source_target_pairs={{0,8},{8,16},{16,24},{24,32},{32,40},{40,48},{48,56},{56,64},{64,7... | collective-permute-start | bytes 6152 | tf_op jit(solution)/shard_map/ppermute | solution.py:19
  499.1 10.5 %collective-permute-start.21 = (bf16[128,8,1]{2,0,1:T(8,128)(2,1)S(1)}, bf16[128,8,1]{2,0,1:T(8,128)(2,1)S(1)}, u32[]{:S(2)}, u32[]{:S(2)}) collective-permute-start(bf16[128,8,1]{2,0,1:T(8,128)(2,1)S(1)} %get-tuple-element.72), channel_id=1, source_target_pairs={{8,0},{16,8},{24,16},{32,24},{40,32},{48,40},{56,48},{64,56},{72,6... | collective-permute-start | bytes 6152 | tf_op jit(solution)/shard_map/ppermute | solution.py:21
  500.1 17.8 %copy-start.19 = (bf16[128,8,1]{2,0,1:T(8,128)(2,1)}, bf16[128,8,1]{2,0,1:T(8,128)(2,1)S(1)}, u32[]{:S(2)}) copy-start(bf16[128,8,1]{2,0,1:T(8,128)(2,1)S(1)} %collective-permute-done.8) | copy-start | bytes 6148
  501.4 25.1 %collective-permute-start.10 = (bf16[128,1,258]{2,0,1:T(8,128)(2,1)}, bf16[128,1,258]{2,0,1:T(8,128)(2,1)}, u32[]{:S(2)}, u32[]{:S(2)}) collective-permute-start(bf16[128,1,258]{2,0,1:T(8,128)(2,1)} %get-tuple-element.41), channel_id=1, source_target_pairs={{0,1},{1,2},{2,3},{3,4},{4,5},{5,6},{6,7},{8,9},{9,10},{10,11},{11... | collective-permute-start | bytes 198152 | tf_op jit(solution)/shard_map/ppermute | solution.py:19
  505.0 21.5 %collective-permute-start.11 = (bf16[128,1,258]{2,0,1:T(8,128)(2,1)}, bf16[128,1,258]{2,0,1:T(8,128)(2,1)}, u32[]{:S(2)}, u32[]{:S(2)}) collective-permute-start(bf16[128,1,258]{2,0,1:T(8,128)(2,1)} %get-tuple-element.40), channel_id=1, source_target_pairs={{1,0},{2,1},{3,2},{4,3},{5,4},{6,5},{7,6},{9,8},{10,9},{11,10},{12... | collective-permute-start | bytes 198152 | tf_op jit(solution)/shard_map/ppermute | solution.py:21
  510.4 30.8 %collective-permute-start.22 = (bf16[128,1,258]{2,0,1:T(8,128)(2,1)}, bf16[128,1,258]{2,0,1:T(8,128)(2,1)S(1)}, u32[]{:S(2)}, u32[]{:S(2)}) collective-permute-start(bf16[128,1,258]{2,0,1:T(8,128)(2,1)} %get-tuple-element.37), channel_id=1, source_target_pairs={{1,0},{2,1},{3,2},{4,3},{5,4},{6,5},{7,6},{9,8},{10,9},{11,10},{12... | collective-permute-start | bytes 198152 | tf_op jit(solution)/shard_map/ppermute | solution.py:21
  511.7 29.5 %collective-permute-start.23 = (bf16[128,1,258]{2,0,1:T(8,128)(2,1)}, bf16[128,1,258]{2,0,1:T(8,128)(2,1)}, u32[]{:S(2)}, u32[]{:S(2)}) collective-permute-start(bf16[128,1,258]{2,0,1:T(8,128)(2,1)} %get-tuple-element.36), channel_id=1, source_target_pairs={{0,1},{1,2},{2,3},{3,4},{4,5},{5,6},{6,7},{8,9},{9,10},{10,11},{11... | collective-permute-start | bytes 198152 | tf_op jit(solution)/shard_map/ppermute | solution.py:19
  (61 other events, 238.3 us)
Sparse Core Ops, SparseCore 0:
  9.7 66.5 all-gather.1
  579.0 150.6 all-reduce.6
where the time goes:
time: 750 us; the launch traced here: 741 us
  blocking collectives  262 us (35%)
  waiting for transfers between devices  218 us (29%)
  local copies, waits for them, and re-layouts  123 us (16%)
  starting transfers between devices  46.1 us (6%)
  matrix products  41.2 us (5%)
  other arithmetic  34.6 us (5%)
  between operations  15.8 us (2%)
    psum x1, waiting for transfers between devices, local(): grad_weight_in = lax.psum(local_in, ('lon', 'lat')) * factor  143 us
    psum x2, blocking collectives, spread_back(): lax.psum((jnp.sum(grouped, 1), jnp.sum(grouped * normed_group, 1)), ('lon...  131 us
    psum x2, blocking collectives, spread_stats(): lax.psum((jnp.sum(grouped, 1), jnp.sum(grouped * grouped, 1)), ('lon', 'l...  131 us
    gather x1, local copies, waits for them, and re-layouts, local(): gathered_pool[interp_src // block_cells, :, interp_src % block_cells]  47.9 us
    all_gather x1, waiting for transfers between devices, local(): column = lax.all_gather(coarse_blocks, 'lat', axis=1, tiled=True)  43.5 us
    ppermute x12, starting transfers between devices, with_halo(): lax.ppermute(tail, axis, [(i, (i + 1) % count) for i in range(ends)])  36.8 us
    ppermute x12, waiting for transfers between devices, with_halo(): lax.ppermute(head, axis, [((i + 1) % count, i) for i in range(ends)])  21.4 us
    slice x13, local copies, waits for them, and re-layouts, transposed(): padded[:, row_shift:row_shift + height, col_shift:col_shift + breadth]  18.8 us
  transfers between devices with their start and end apart: 26, of which 12 were waited for; matrix products, arithmetic and copies ran while one was open for 7% of the time, Pallas kernels for 0%

commit v1 on v0

v1 whole, which is shorter than its diff:
```python
import jax
import jax.numpy as jnp
from jax import lax
from jax.experimental import pallas as pl
from jax.experimental.pallas import tpu as pltpu
from jax.sharding import PartitionSpec as P

C = 128
CC = 40
G = 32
H = 8
W = 256
N = H * W
NP = N + 2 * W
BS = 256
SLOT = 8
NLON = 16
NLAT = 8
CELLS = 64 * 4096
MEMBERS = (C // G) * CELLS
FACTOR = CELLS ** -0.5
EPS = 1e-05
ROWS_IN = 96
ROWS_OM = 144
F32 = jnp.float32
BF16 = jnp.bfloat16
MESH = pl.DeviceIdType.MESH
FEAT, COT, COND, POOL, MERG, GMID, GIN = range(7)
HOPS = (0, 1, 2, 1)
OTHERS = sorted(
    [(a, b, c, d) for a in range(4) for b in range(4) for c in range(4) for d in range(2) if (a, b, c, d) != (0, 0, 0, 0)],
    key=lambda o: -(HOPS[o[0]] + HOPS[o[1]] + HOPS[o[2]]),
)
AROUND = [(a, b) for a in (-1, 0, 1) for b in (-1, 0, 1) if (a, b) != (0, 0)]


def dot(a, b):
    return lax.dot_general(a, b, (((1,), (0,)), ((), ())), preferred_element_type=F32)


def dot_nt(a, b):
    return lax.dot_general(a, b, (((1,), (1,)), ((), ())), preferred_element_type=F32)


def sigmoid(v):
    return 1.0 / (1.0 + jnp.exp(-v))


def kernel(
    feat, cot, blocks, table, src, wt, w_in, w_mid, w_out, gain_in, bias_in, gain_mid, bias_mid,
    out, gfeat, g_in, g_om,
    fc, relay, pool_s, pool_r, onehot, fid, fwt, acc, condf, hidden, gmerged, slope, act, merged, gin, up,
    x3f, x3c, x3m, x3g, x3cond, wf, wc, wo, wm, wt_out, wt_mid, wt_in,
    hr, hc, edge_l, edge_r, chr_, chc, cedge_l, cedge_r, pooled, gmid, near_p, near_g, im_p, im_g,
    a1, gw_in, s_in, s_om, core_in, core_om, half_in, half_om, r1_in, r1_om, r2_in, r2_om, full_in, full_om,
    sem_ps, sem_pr, sem_hs, sem_hr, sem_a, sem_b,
):
    lon = lax.axis_index("lon")
    lat = lax.axis_index("lat")

    def at(dlat, dlon):
        return {"lon": lax.rem(lon + dlon + NLON, NLON), "lat": lat + dlat}

    def has_lat(d):
        if d == 0:
            return None
        return jnp.logical_and(lat + d >= 0, lat + d < NLAT)

    def guarded(cond, fn):
        if cond is None:
            fn()
        else:
            pl.when(cond)(fn)

    finish = []

    def send(cond, source, dest, s_sem, r_sem, device):
        copy = pltpu.make_async_remote_copy(
            src_ref=source, dst_ref=dest, send_sem=s_sem, recv_sem=r_sem,
            device_id=device, device_id_type=MESH,
        )
        guarded(cond, copy.start)
        finish.append((cond, copy.wait_send))

    def arrive(ref, sem):
        pltpu.make_async_copy(ref, ref, sem).wait()

    barrier = pltpu.get_barrier_semaphore()

    core = lax.rem(lon, 2)
    chip = lon // 2
    x = lon // 4
    z = lat // 2
    y = lax.rem(chip, 2) * 2 + lax.rem(lat, 2)
    lon_of = {}
    lat_of = {}
    for oy in range(4):
        y2 = lax.rem(y + oy, 4)
        for oc in range(2):
            for ox in range(4):
                lon_of[ox, oy, oc] = (lax.rem(x + ox, 4) * 2 + y2 // 2) * 2 + (core if oc == 0 else 1 - core)
        for oz in range(4):
            lat_of[oz, oy] = lax.rem(z + oz, 4) * 2 + lax.rem(y2, 2)

    def everyone(act_on):
        for ox, oy, oz, oc in OTHERS:
            act_on({"lon": lon_of[ox, oy, oc], "lat": lat_of[oz, oy]})

    everyone(lambda peer: pl.semaphore_signal(barrier, inc=1, device_id=peer, device_id_type=MESH))

    def relaid(ref, base):
        cells = ref[...].astype(F32).reshape(C * H, W)
        for side in range(2):
            relay[side * C * H:(side + 1) * C * H] = cells[:, side * 128:(side + 1) * 128]
            for r in range(H):
                where = slice(r * W + side * 128, r * W + (side + 1) * 128)
                fc[base:base + C, where] = relay[pl.ds(side * C * H + r, C, stride=H), :].astype(BF16)

    relaid(feat, 0)
    relaid(cot, C)

    gaps = [0, 1, -1, 2, -2, 3, -3, 4, -4]

    def pack(k, dest):
        for s2 in range(0, 4, 2):
            for half in range(2):
                one = jnp.maximum(table[0, lat, lat + gaps[k], 2 * s2 + half], 0)
                two = jnp.maximum(table[0, lat, lat + gaps[k], 2 * s2 + 2 + half], 0)
                both = jnp.concatenate([blocks[0, one].astype(F32), blocks[0, two].astype(F32)], axis=0)
                dest[s2 * CC:(s2 + 2) * CC, half * BS:(half + 1) * BS] = both.astype(BF16)

    pack(0, pool_r.at[0])
    for k in range(1, 9):
        guarded(has_lat(gaps[k]), lambda k=k: pack(k, pool_s.at[k]))

    lane = lax.broadcasted_iota(jnp.int32, (C, 128), 1)

    def edge_columns(ref, offset, chans, left, right):
        lanes = lax.broadcasted_iota(jnp.int32, (chans, 128), 1)
        to_l = jnp.zeros((chans, 128), F32)
        to_r = jnp.zeros((chans, 128), F32)
        for r in range(H):
            base = offset + r * W
            first = ref[:, base:base + 128].astype(F32)
            last = ref[:, base + 128:base + 256].astype(F32)
            to_l = jnp.where(lanes == r + 1, first[:, 0:1], to_l)
            to_r = jnp.where(lanes == r + 1, last[:, 127:128], to_r)
        left[...] = to_l.astype(left.dtype)
        right[...] = to_r.astype(right.dtype)

    edge_columns(fc.at[0:C], 0, C, edge_l.at[FEAT], edge_r.at[FEAT])
    edge_columns(fc.at[C:2 * C], 0, C, edge_l.at[COT], edge_r.at[COT])

    pl.semaphore_wait(barrier, NLAT * NLON - 1)

    def send_fine(f, ref, offset, rows_at, cols_at, left, right):
        send(has_lat(-1), ref.at[:, offset:offset + W], rows_at.at[1], sem_hs.at[f, 0], sem_hr.at[f, 1], at(-1, 0))
        send(has_lat(1), ref.at[:, offset + N - W:offset + N], rows_at.at[0], sem_hs.at[f, 1], sem_hr.at[f, 0], at(1, 0))
        for d in (0, -1, 1):
            send(has_lat(d), right, cols_at.at[1 - d], sem_hs.at[f, 3 + d], sem_hr.at[f, 3 - d], at(d, 1))
            send(has_lat(d), left, cols_at.at[4 - d], sem_hs.at[f, 6 + d], sem_hr.at[f, 6 - d], at(d, -1))

    def expect(cond, ref, sem):
        if cond is None:
            arrive(ref, sem)
            return

        @pl.when(cond)
        def _():
            arrive(ref, sem)

        @pl.when(jnp.logical_not(cond))
        def _():
            ref[...] = jnp.zeros(ref.shape, ref.dtype)

    def wait_fine(f, rows_at, cols_at):
        expect(has_lat(-1), rows_at.at[0], sem_hr.at[f, 0])
        expect(has_lat(1), rows_at.at[1], sem_hr.at[f, 1])
        for d in (0, -1, 1):
            expect(has_lat(d), cols_at.at[1 + d], sem_hr.at[f, 3 + d])
            expect(has_lat(d), cols_at.at[4 + d], sem_hr.at[f, 6 + d])

    for k in range(1, 9):
        back = gaps.index(-gaps[k])
        send(has_lat(gaps[k]), pool_s.at[k], pool_r.at[back], sem_ps.at[k], sem_pr.at[back], at(gaps[k], 0))
    send_fine(FEAT, fc.at[0:C], 0, hr.at[FEAT], hc.at[FEAT], edge_l.at[FEAT], edge_r.at[FEAT])
    send_fine(COT, fc.at[C:2 * C], 0, hr.at[COT], hc.at[COT], edge_l.at[COT], edge_r.at[COT])

    def make_onehot(j, _):
        m = j // H
        r = lax.rem(j, H)
        cells = src[m, pl.ds(r, 1), :]
        low = lax.rem(cells, 2 * BS)
        rows = lax.broadcasted_iota(jnp.int32, (2 * BS, W), 0)
        where = pl.ds(pl.multiple_of(j * W, W), W)
        onehot[:, where] = jnp.where(rows == low, 1.0, 0.0).astype(BF16)
        fid[:, where] = cells // (2 * BS)
        fwt[:, where] = wt[m, pl.ds(r, 1), :]
        return 0

    lax.fori_loop(0, 2 * H, make_onehot, 0)

    for r in range(H):
        small = lax.broadcasted_iota(jnp.int32, (C, W), 0)
        cell = lax.broadcasted_iota(jnp.int32, (C, W), 1)
        up[:, r * W:(r + 1) * W] = jnp.where(small == (r // 4) * 64 + cell // 4, 1.0, 0.0).astype(BF16)

    def turn(t):
        return t.astype(F32).T.astype(BF16)

    for a in range(3):
        rows = []
        for b in range(3):
            t = 3 * a + b
            wf[a, :, b * C:(b + 1) * C] = turn(w_in[t, 0:C, :])
            wo[a, :, b * C:(b + 1) * C] = w_out[t]
            wm[:, t * C:(t + 1) * C] = w_mid[t]
            rows.append(w_in[t, C:C + CC, :].astype(F32))
        wc[a] = jnp.concatenate(rows + [jnp.zeros((8, C), F32)], axis=0).T.astype(BF16)

    def turn_out():
        for t in range(9):
            wt_out[t // 3, :, (t % 3) * C:(t % 3 + 1) * C] = turn(w_out[8 - t])

    def turn_rest():
        for t in range(9):
            wt_mid[:, t * C:(t + 1) * C] = turn(w_mid[8 - t])
            wt_in[t // 3, :, (t % 3) * C:(t % 3 + 1) * C] = w_in[8 - t, 0:C, :]

    def left_right(r, cols_at):
        if r == 0:
            return cols_at[0].astype(F32)[:, 8:9], cols_at[3].astype(F32)[:, 8:9]
        if r == H + 1:
            return cols_at[2].astype(F32)[:, 1:2], cols_at[5].astype(F32)[:, 1:2]
        return cols_at[1].astype(F32)[:, r:r + 1], cols_at[4].astype(F32)[:, r:r + 1]

    def shifted(v, r, cols_at):
        chans = v.shape[0]
        at_lane = lax.broadcasted_iota(jnp.int32, (chans, W), 1)
        first, last = left_right(r, cols_at)
        before = jnp.where(at_lane == 0, first, pltpu.roll(v, 1, 1))
        after = jnp.where(at_lane == W - 1, last, pltpu.roll(v, W - 1, 1))
        return before, after

    def build(x3, ref, rows_at, cols_at):
        for r in range(H + 2):
            if r == 0:
                v = rows_at[0]
            elif r == H + 1:
                v = rows_at[1]
            else:
                v = ref[:, (r - 1) * W:r * W]
            before, after = shifted(v.astype(F32), r, cols_at)
            x3[0:C, r * W:(r + 1) * W] = before.astype(BF16)
            x3[C:2 * C, r * W:(r + 1) * W] = v
            x3[2 * C:3 * C, r * W:(r + 1) * W] = after.astype(BF16)

    STEP = 512

    def conv(weights, x3, use):
        def body(j, _):
            total = None
            for a in range(3):
                start = pl.multiple_of(j * STEP + a * W, W)
                part = dot(weights[a], x3[:, pl.ds(start, STEP)])
                total = part if total is None else total + part
            use(pl.ds(pl.multiple_of(j * STEP, STEP), STEP), total)
            return 0

        lax.fori_loop(0, N // STEP, body, 0)

    def put(ref):
        def use(where, v):
            ref[:, where] = v

        return use

    wait_fine(FEAT, hr.at[FEAT], hc.at[FEAT])
    build(x3f, fc.at[0:C], hr.at[FEAT], hc.at[FEAT])
    conv(wf, x3f, put(hidden))
    turn_out()
    wait_fine(COT, hr.at[COT], hc.at[COT])
    build(x3c, fc.at[C:2 * C], hr.at[COT], hc.at[COT])
    conv(wt_out, x3c, put(gmerged))

    def halves(v):
        high = v.astype(BF16)
        return high, (v - high.astype(F32)).astype(BF16)

    high, low = halves(gmerged[...])
    gsmall = dot_nt(high, up[...]) + dot_nt(low, up[...])

    acc[...] = jnp.zeros(acc.shape, F32)

    def interp(k, _):
        gap = jnp.where(lax.rem(k, 2) == 1, (k + 1) // 2, -(k // 2))
        owner = lat + gap

        @pl.when(jnp.logical_and(owner >= 0, owner < NLAT))
        def _():
            @pl.when(k > 0)
            def _():
                arrive(pool_r.at[k], sem_pr.at[k])

            products = dot(pool_r[k], onehot[...])
            total = acc[...]
            for s2 in range(4):
                mask = jnp.where(fid[...] == owner * 4 + s2, fwt[...], 0.0)
                total = total + products[s2 * CC:(s2 + 1) * CC] * mask
            acc[...] = total

        return 0

    lax.fori_loop(0, 9, interp, 0)

    blended = acc[:, 0:N] + acc[:, N:2 * N]
    condf[:, W:W + N] = blended.astype(BF16).astype(F32)
    edge_columns(condf, W, CC, cedge_l, cedge_r)
    send_fine(COND, condf, W, chr_, chc, cedge_l, cedge_r)
    wait_fine(COND, chr_, chc)
    for r in range(H + 2):
        if r == 0:
            v = chr_[0]
        elif r == H + 1:
            v = chr_[1]
        else:
            v = condf[:, r * W:(r + 1) * W]
        before, after = shifted(v, r, chc)
        stacked = jnp.concatenate([before, v, after, jnp.zeros((8, W), F32)], axis=0)
        x3cond[:, r * W:(r + 1) * W] = stacked.astype(BF16)

    def add_hidden(where, v):
        hidden[:, where] = hidden[:, where] + v

    conv(wc, x3cond, add_hidden)

    chan = lax.broadcasted_iota(jnp.int32, (C, C), 0)
    other = lax.broadcasted_iota(jnp.int32, (C, C), 1)
    eye = chan == other
    to_first = jnp.where(other == chan // (C // G), 1.0, 0.0)
    to_second = jnp.where(other == G + chan // (C // G), 1.0, 0.0)
    me = lat * NLON + lon

    def to_col(row):
        return jnp.sum(jnp.where(eye, row, 0.0), axis=1, keepdims=True)

    def all_sum(k, first, second, beside=None):
        one = jnp.sum(first, axis=1, keepdims=True)
        two = jnp.sum(second, axis=1, keepdims=True)
        mine = a1.at[k, pl.ds(me, 1)]
        a1[k, pl.ds(me, 1), :] = jnp.sum(one * to_first + two * to_second, axis=0, keepdims=True)

        def share(peer):
            pltpu.make_async_remote_copy(
                src_ref=mine, dst_ref=mine, send_sem=sem_a.at[k, 0], recv_sem=sem_a.at[k, 1],
                device_id=peer, device_id_type=MESH,
            ).start()

        everyone(share)
        if beside is not None:
            beside()
        rest = a1.at[k, pl.ds(0, NLAT * NLON - 1)]
        arrive(rest, sem_a.at[k, 1])
        finish.append((None, lambda: arrive(rest, sem_a.at[k, 0])))
        total = jnp.sum(a1[k], axis=0, keepdims=True)
        return (
            jnp.sum(total * to_first, axis=1, keepdims=True),
            jnp.sum(total * to_second, axis=1, keepdims=True),
        )

    def norm_terms(sums, squares, members):
        average = sums / members
        variance = squares / members - average * average
        return average, lax.rsqrt(variance + EPS)

    s = jnp.zeros((C, 128), F32)
    q = jnp.zeros((C, 128), F32)
    for j in range(N // 128):
        v = hidden[:, j * 128:(j + 1) * 128]
        s = s + v
        q = q + v * v
    sums, squares = all_sum(0, s, q, turn_rest)
    avg_in, inv_in = norm_terms(sums, squares, MEMBERS)
    g1 = to_col(gain_in[...])
    b1 = to_col(bias_in[...])
    g2 = to_col(gain_mid[...])
    b2 = to_col(bias_mid[...])

    def activate(j, _):
        where = pl.ds(pl.multiple_of(j * W, W), W)
        affine = g1 * ((hidden[:, where] - avg_in) * inv_in) + b1
        act[:, where] = (affine * sigmoid(affine)).astype(BF16)
        return 0

    lax.fori_loop(0, H, activate, 0)

    def send_coarse(f, ref, near):
        for i, (dlat, dlon) in enumerate(AROUND):
            send(has_lat(dlat), ref, near.at[7 - i], sem_hs.at[f, i], sem_hr.at[f, 7 - i], at(dlat, dlon))

    def wait_coarse(f, near):
        for i, (dlat, dlon) in enumerate(AROUND):
            expect(has_lat(dlat), near.at[i], sem_hr.at[f, i])

    def build_coarse(im, ref, near):
        def column(up_, mid_, down_):
            u, m, d = up_.astype(F32), mid_.astype(F32), down_.astype(F32)
            over = jnp.where(lane < 64, pltpu.roll(u, 64, 1), pltpu.roll(m, 64, 1))
            under = jnp.where(lane < 64, pltpu.roll(m, 64, 1), pltpu.roll(d, 64, 1))
            return over, m, under

        lefts = column(near[0], near[3], near[5])
        mids = column(near[1], ref[...], near[6])
        rights = column(near[2], near[4], near[7])
        for a in range(3):
            before = jnp.where(lane % 64 == 0, pltpu.roll(lefts[a], 65, 1), pltpu.roll(mids[a], 1, 1))
            after = jnp.where(lane % 64 == 63, pltpu.roll(rights[a], 63, 1), pltpu.roll(mids[a], 127, 1))
            im[(3 * a) * C:(3 * a + 1) * C] = before.astype(BF16)
            im[(3 * a + 1) * C:(3 * a + 2) * C] = mids[a].astype(BF16)
            im[(3 * a + 2) * C:(3 * a + 3) * C] = after.astype(BF16)

    pooled[...] = (dot_nt(act[...], up[...]) * (1.0 / 16.0)).astype(BF16)
    send_coarse(POOL, pooled, near_p)
    wait_coarse(POOL, near_p)
    build_coarse(im_p, pooled, near_p)
    hidden_mid = dot(wm[...], im_p[...])
    sums, squares = all_sum(1, hidden_mid, hidden_mid * hidden_mid)
    avg_mid, inv_mid = norm_terms(sums, squares, MEMBERS // 16)
    normed_mid = (hidden_mid - avg_mid) * inv_mid
    affine_mid = g2 * normed_mid + b2
    sig = sigmoid(affine_mid)
    act_mid = (affine_mid * sig).astype(BF16)
    slope_mid = gsmall * sig * (1.0 + affine_mid * (1.0 - sig)) * g2

    def send_merged():
        for r in range(H):
            where = slice(r * W, (r + 1) * W)
            merged[:, where] = (act[:, where].astype(F32) + dot(act_mid, up[:, where])).astype(BF16)
        edge_columns(merged, 0, C, edge_l.at[MERG], edge_r.at[MERG])
        send_fine(MERG, merged, 0, hr.at[MERG], hc.at[MERG], edge_l.at[MERG], edge_r.at[MERG])

    sum_e, sum_en = all_sum(2, slope_mid, slope_mid * normed_mid, send_merged)
    mean_e = sum_e / (MEMBERS // 16)
    mean_en = sum_en / (MEMBERS // 16)
    gmid[...] = ((slope_mid - mean_e - normed_mid * mean_en) * inv_mid).astype(BF16)
    send_coarse(GMID, gmid, near_g)
    g_mid_w = dot_nt(gmid[...], im_p[...])
    for t in range(9):
        s_om[t * C:(t + 1) * C] = g_mid_w[:, t * C:(t + 1) * C].astype(BF16)
    wait_coarse(GMID, near_g)
    build_coarse(im_g, gmid, near_g)
    gpooled = dot(wt_mid[...], im_g[...]) * (1.0 / 16.0)
    high, low = halves(gpooled)

    def slopes(j, carry):
        s, q = carry
        where = pl.ds(pl.multiple_of(j * W, W), W)
        gact = gmerged[:, where] + dot(high, up[:, where]) + dot(low, up[:, where])
        normed = (hidden[:, where] - avg_in) * inv_in
        affine = g1 * normed + b1
        sig = sigmoid(affine)
        e = gact * sig * (1.0 + affine * (1.0 - sig)) * g1
        slope[:, where] = e
        en = e * normed
        return s + e[:, 0:128] + e[:, 128:256], q + en[:, 0:128] + en[:, 128:256]

    s, q = lax.fori_loop(0, H, slopes, (jnp.zeros((C, 128), F32), jnp.zeros((C, 128), F32)))

    jobs = {
        0: (ROWS_OM, s_om, core_om, half_om, r1_om, r2_om, full_om),
        1: (ROWS_IN, s_in, core_in, half_in, r1_in, r2_in, full_in),
    }
    partner = {"lon": lon + 1 - 2 * core, "lat": lat}

    def pieces(ref, n):
        return ref.at[pl.ds(0, n)]

    def hand(k, step, source, dest, peer):
        pltpu.make_async_remote_copy(
            src_ref=source, dst_ref=dest, send_sem=sem_b.at[k, 2 * step], recv_sem=sem_b.at[k, 2 * step + 1],
            device_id=peer, device_id_type=MESH,
        ).start()

    def along_lon(d):
        return lax.rem(chip + d, NLON // 2)

    def cores(k):
        rows, s_ref, got = jobs[k][:3]
        part = pl.ds(pl.multiple_of((1 - core) * 8 * rows, 16), 8 * rows)
        hand(k, 0, s_ref.at[part], got, partner)
        finish.append((None, lambda: arrive(got, sem_b.at[k, 0])))

    def scatter(k):
        rows, s_ref, got, half, r1 = jobs[k][:5]
        arrive(got, sem_b.at[k, 1])
        part = pl.ds(pl.multiple_of(core * 8 * rows, 16), 8 * rows)
        half[...] = (s_ref[part, :].astype(F32) + got[...].astype(F32)).astype(BF16)
        for d in range(1, 8):
            to = along_lon(d)
            hand(k, 1, half.at[pl.ds(pl.multiple_of(to * rows, 16), rows)], r1.at[chip], {"lon": to * 2 + core, "lat": lat})
        r1[chip] = half[pl.ds(pl.multiple_of(chip * rows, 16), rows), :]
        finish.append((None, lambda: arrive(pieces(r1, 7), sem_b.at[k, 2])))

    def added(ref):
        total = ref[0].astype(F32)
        for i in range(1, 8):
            total = total + ref[i].astype(F32)
        return total.astype(BF16)

    def middle(k):
        r1, r2 = jobs[k][4:6]
        arrive(pieces(r1, 7), sem_b.at[k, 3])
        r2[lat] = added(r1)
        for d in range(1, NLAT):
            hand(k, 2, r2.at[lat], r2.at[lat], {"lon": lon, "lat": lax.rem(lat + d, NLAT)})
        finish.append((None, lambda: arrive(pieces(r2, 7), sem_b.at[k, 4])))

    def gather(k):
        r2, full = jobs[k][5:7]
        arrive(pieces(r2, 7), sem_b.at[k, 5])
        full[core, chip] = added(r2)
        for d in range(1, 8):
            hand(k, 3, full.at[core, chip], full.at[core, chip], {"lon": along_lon(d) * 2 + core, "lat": lat})
        finish.append((None, lambda: arrive(pieces(full.at[core], 7), sem_b.at[k, 6])))

    def exchange(k):
        full = jobs[k][6]
        arrive(pieces(full.at[core], 7), sem_b.at[k, 7])
        hand(k, 4, full.at[core], full.at[core], partner)
        finish.append((None, lambda: arrive(full.at[core], sem_b.at[k, 8])))

    def complete(k, result):
        full = jobs[k][6]
        arrive(full.at[1 - core], sem_b.at[k, 9])
        result[...] = full[...]

    def beside_slopes():
        wait_fine(MERG, hr.at[MERG], hc.at[MERG])
        build(x3m, merged, hr.at[MERG], hc.at[MERG])
        for a in range(3):
            part = dot_nt(fc[C:2 * C], x3m[:, a * W:a * W + N])
            for b in range(3):
                t = 9 + 3 * a + b
                s_om[t * C:(t + 1) * C] = part[:, b * C:(b + 1) * C].astype(BF16)
        cores(0)
        scatter(0)

    sum_e, sum_en = all_sum(3, s, q, beside_slopes)
    mean_e = sum_e / MEMBERS
    mean_en = sum_en / MEMBERS

    def finish_in(j, _):
        where = pl.ds(pl.multiple_of(j * W, W), W)
        normed = (hidden[:, where] - avg_in) * inv_in
        gin[:, where] = ((slope[:, where] - mean_e - normed * mean_en) * inv_in).astype(BF16)
        return 0

    lax.fori_loop(0, H, finish_in, 0)

    edge_columns(gin, 0, C, edge_l.at[GIN], edge_r.at[GIN])
    send_fine(GIN, gin, 0, hr.at[GIN], hc.at[GIN], edge_l.at[GIN], edge_r.at[GIN])
    taps = C + CC
    for a in range(3):
        part = dot_nt(x3f[:, a * W:a * W + N], gin[...])
        more = dot_nt(x3cond[:, a * W:a * W + N], gin[...])
        for b in range(3):
            t = 3 * a + b
            gw_in[t * taps:t * taps + C] = part[b * C:(b + 1) * C]
            gw_in[t * taps + C:(t + 1) * taps] = more[b * CC:(b + 1) * CC]
    gw_in[9 * taps:] = jnp.zeros((16 * ROWS_IN - 9 * taps, C), F32)
    s_in[...] = gw_in[...].astype(BF16)
    cores(1)
    middle(0)
    scatter(1)

    def put_out(where, v):
        out[:, where] = (fc[0:C, where].astype(F32) + v).astype(BF16)

    conv(wo, x3m, put_out)
    gather(0)
    middle(1)
    wait_fine(GIN, hr.at[GIN], hc.at[GIN])
    build(x3g, gin, hr.at[GIN], hc.at[GIN])

    def put_feat(where, v):
        gfeat[:, where] = (fc[C:2 * C, where].astype(F32) + v).astype(BF16)

    conv(wt_in, x3g, put_feat)
    gather(1)
    exchange(0)
    complete(0, g_om)
    exchange(1)
    complete(1, g_in)
    for cond, wait in finish:
        guarded(cond, wait)


def local(
    features, coarse_blocks, send_table, interp_src, interp_wt, weight_in, weight_mid, weight_out,
    gain_in, bias_in, gain_mid, bias_mid, cotangent,
):
    vmem = pl.BlockSpec(memory_space=pltpu.VMEM)
    smem = pl.BlockSpec(memory_space=pltpu.SMEM)
    V = pltpu.VMEM
    scratch = [
        V((2 * C, N), BF16), V((2 * C * H, 128), F32),
        V((9, 4 * CC, 2 * BS), BF16), V((9, 4 * CC, 2 * BS), BF16), V((2 * BS, 2 * N), BF16),
        V((1, 2 * N), jnp.int32), V((1, 2 * N), F32),
        V((CC, 2 * N), F32), V((CC, NP), F32), V((C, N), F32), V((C, N), F32), V((C, N), F32),
        V((C, N), BF16), V((C, N), BF16), V((C, N), BF16), V((C, N), BF16),
        V((3 * C, NP), BF16), V((3 * C, NP), BF16), V((3 * C, NP), BF16), V((3 * C, NP), BF16), V((C, NP), BF16),
        V((3, C, 3 * C), BF16), V((3, C, C), BF16), V((3, C, 3 * C), BF16), V((C, 9 * C), BF16),
        V((3, C, 3 * C), BF16), V((C, 9 * C), BF16), V((3, C, 3 * C), BF16),
        V((7, 2, C, W), BF16), V((7, 6, C, 128), BF16), V((7, C, 128), BF16), V((7, C, 128), BF16),
        V((2, CC, W), F32), V((6, CC, 128), F32), V((CC, 128), F32), V((CC, 128), F32),
        V((C, 128), BF16), V((C, 128), BF16), V((8, C, 128), BF16), V((8, C, 128), BF16),
        V((9 * C, 128), BF16), V((9 * C, 128), BF16),
        V((4, NLAT * NLON, C), F32), V((16 * ROWS_IN, C), F32),
        V((16 * ROWS_IN, C), BF16), V((16 * ROWS_OM, C), BF16), V((8 * ROWS_IN, C), BF16), V((8 * ROWS_OM, C), BF16),
        V((8 * ROWS_IN, C), BF16), V((8 * ROWS_OM, C), BF16), V((8, ROWS_IN, C), BF16), V((8, ROWS_OM, C), BF16),
        V((8, ROWS_IN, C), BF16), V((8, ROWS_OM, C), BF16), V((2, 8, ROWS_IN, C), BF16), V((2, 8, ROWS_OM, C), BF16),
        pltpu.SemaphoreType.DMA((9,)), pltpu.SemaphoreType.DMA((9,)),
        pltpu.SemaphoreType.DMA((7, 8)), pltpu.SemaphoreType.DMA((7, 8)),
        pltpu.SemaphoreType.DMA((4, 2)), pltpu.SemaphoreType.DMA((2, 10)),
    ]
    out, gfeat, g_in, g_om = pl.pallas_call(
        kernel,
        out_shape=(
            jax.ShapeDtypeStruct((C, N), BF16), jax.ShapeDtypeStruct((C, N), BF16),
            jax.ShapeDtypeStruct((2, 8, ROWS_IN, C), BF16), jax.ShapeDtypeStruct((2, 8, ROWS_OM, C), BF16),
        ),
        in_specs=[vmem, vmem, vmem, smem] + [vmem] * 9,
        out_specs=(vmem,) * 4,
        scratch_shapes=scratch,
        compiler_params=pltpu.CompilerParams(
            collective_id=0, has_side_effects=True, vmem_limit_bytes=56 * 1024 * 1024
        ),
    )(
        features, cotangent, coarse_blocks, send_table, interp_src, interp_wt, jnp.swapaxes(weight_in, 1, 2), weight_mid, weight_out,
        gain_in.reshape(1, C), bias_in.reshape(1, C), gain_mid.reshape(1, C), bias_mid.reshape(1, C),
    )
    shape = features.shape
    grad_in = g_in.reshape(16 * ROWS_IN, C)[:9 * (C + CC)].reshape(9, C + CC, C).astype(F32) * FACTOR
    grad_in = jnp.swapaxes(grad_in, 1, 2)
    taps = g_om.reshape(18, C, C)
    grad_mid = taps[:9].astype(F32) * FACTOR
    grad_out = taps[9:].astype(F32) * FACTOR
    return out.reshape(shape), gfeat.reshape(shape), grad_in, grad_mid, grad_out


def solution(mesh):
    tile = P(None, "lat", "lon")
    in_specs = (
        tile, P("lon", "lat", None, None), P("lon", None, None, None), tile, tile,
        P(), P(), P(), P(), P(), P(), P(), tile,
    )
    out_specs = (tile, tile, P(), P(), P())
    return jax.shard_map(local, mesh=mesh, in_specs=in_specs, out_specs=out_specs, check_vma=False)
```

time: 750 us -> 131 us (0.17); the launches traced: 741 us -> 131 us
  blocking collectives: 262 us -> 0 us
  waiting for transfers between devices: 218 us -> 0 us
  Pallas kernels: 0 us -> 125 us
  local copies, waits for them, and re-layouts: 123 us -> 2.33 us
  starting transfers between devices: 46.1 us -> 0 us
  matrix products: 41.2 us -> 0 us
  other arithmetic: 34.6 us -> 3.12 us
  between operations: 15.8 us -> 0.66 us
    psum x4 -> x0, blocking collectives: 262 us -> none  [the longest x2 131 us: spread_back(): lax.psum((jnp.sum(grouped, 1), jnp.sum(grouped * normed_group, 1)), ('lon...]
    psum x1 -> x0, waiting for transfers between devices: 143 us -> none  [local(): grad_weight_in = lax.psum(local_in, ('lon', 'lat')) * factor]
    pallas_call x0 -> x1, Pallas kernels: none -> 125 us  [local(): pl.pallas_call(kernel, out_shape=(jax.ShapeDtypeStruct((C, N), BF16), jax...]
    gather x2 -> x0, local copies, waits for them, and re-layouts: 50.3 us -> none  [the longest x1 47.9 us: local(): gathered_pool[interp_src // block_cells, :, interp_src % block_cells]]
    ppermute x24 -> x0, starting transfers between devices: 46 us -> none  [the longest x12 36.8 us: with_halo(): lax.ppermute(tail, axis, [(i, (i + 1) % count) for i in range(ends)])]
    all_gather x1 -> x0, waiting for transfers between devices: 43.5 us -> none  [local(): column = lax.all_gather(coarse_blocks, 'lat', axis=1, tiled=True)]
    dot_general x81 -> x0, matrix products: 41.2 us -> none  [the longest x27 16.2 us: correlate(): lax.dot_general(flattened, window, (((1,), (1,)), ((), ())), preferred_el...]
    slice x32 -> x0, local copies, waits for them, and re-layouts: 35.8 us -> none  [the longest x13 18.8 us: transposed(): padded[:, row_shift:row_shift + height, col_shift:col_shift + breadth]]
  transfers between devices with their start and end apart: 26 -> 0, of which waited for: 12 -> 0; matrix products, arithmetic and copies ran while one was open for 7% -> 0% of each run, Pallas kernels for 0% -> 0%
where the time goes in v1:
time: 131 us
  Pallas kernels  125 us (95%)
  other arithmetic  3.12 us (2%)
  local copies, waits for them, and re-layouts  2.33 us (2%)
    pallas_call x1, Pallas kernels, local(): pl.pallas_call(kernel, out_shape=(jax.ShapeDtypeStruct((C, N), BF16), jax...  125 us

profile of v1, /device:TPU:1, one launch (start us, length us, event | category | flops | bytes accessed | tf_op | source)
XLA Modules:
  0.0 130.6 jit_solution(5958761709645297628)
XLA Ops:
  0.6 124.5 %shard_map.164 = (bf16[128,2048]{1,0:T(8,128)(2,1)}, bf16[128,2048]{1,0:T(8,128)(2,1)}, bf16[2,8,96,128]{3,2,1,0:T(8,128)(2,1)}, bf16[2,8,144,128]{3,2,1,0:T(8,128)(2,1)}) custom-call(bf16[128,8,256]{2,1,0:T(8,128)(2,1)} %feat.1, bf16[128,8,256]{2,1,0:T(8,128)(2,1)} %cot.1, bf16[1,16,40,256]{3,2,1,0:T(8,128)(2,1)} %blocks.1, s32[1,8,8,8]{3,2,1,0:T(8,128)} %table.1, ...), custom_call_target="tpu_custom_call" | custom-call | tf_op jit(solution)/shard_map/pallas_call | solution.py:626
  125.2 0.0 copy-start.2
  125.2 2.2 %convert_multiply_fusion.1 = (f32[1,8,144,128]{3,2,1,0:T(8,128)}, f32[1,8,144,128]{3,2,1,0:T(8,128)}) fusion(bf16[2,8,144,128]{3,2,1,0:T(8,128)(2,1)} %get-tuple-element.12), kind=kLoop, calls=%fused_computation.1 | loop fusion | flops 589824 | bytes 1769472 | tf_op jit(solution)/shard_map/mul | solution.py:647
  127.4 0.0 copy-done.2
  127.4 0.0 copy-start.1
  127.4 0.9 convert_multiply_fusion
  128.3 0.3 copy-done.1
  128.6 0.0 copy-start
  128.6 0.9 copy.18
  129.5 0.2 copy-done
  129.7 0.9 copy.19
Async XLA Ops:
  125.2 2.2 %copy-start.2 = (bf16[2,8,96,128]{3,2,1,0:T(8,128)(2,1)S(1)}, bf16[2,8,96,128]{3,2,1,0:T(8,128)(2,1)}, u32[]{:S(2)}) copy-start(bf16[2,8,96,128]{3,2,1,0:T(8,128)(2,1)} %get-tuple-element.11) | copy-start | bytes 1179652
  127.4 1.3 copy-start.1
  128.6 1.1 copy-start

commit v2 on v1

--- a/solution.py
+++ b/solution.py
@@ -22,6 +22,9 @@
 EPS = 1e-05
 ROWS_IN = 96
 ROWS_OM = 144
+AT_OM = 4 * H * C
+AT_IN = AT_OM + 16 * ROWS_OM
+ROWS = AT_IN + 16 * ROWS_IN
 F32 = jnp.float32
 BF16 = jnp.bfloat16
 MESH = pl.DeviceIdType.MESH
@@ -31,7 +34,6 @@
     [(a, b, c, d) for a in range(4) for b in range(4) for c in range(4) for d in range(2) if (a, b, c, d) != (0, 0, 0, 0)],
     key=lambda o: -(HOPS[o[0]] + HOPS[o[1]] + HOPS[o[2]]),
 )
-AROUND = [(a, b) for a in (-1, 0, 1) for b in (-1, 0, 1) if (a, b) != (0, 0)]
 
 
 def dot(a, b):
@@ -48,10 +50,10 @@
 
 def kernel(
     feat, cot, blocks, table, src, wt, w_in, w_mid, w_out, gain_in, bias_in, gain_mid, bias_mid,
-    out, gfeat, g_in, g_om,
+    res,
     fc, relay, pool_s, pool_r, onehot, fid, fwt, acc, condf, hidden, gmerged, slope, act, merged, gin, up,
     x3f, x3c, x3m, x3g, x3cond, wf, wc, wo, wm, wt_out, wt_mid, wt_in,
-    hr, hc, edge_l, edge_r, chr_, chc, cedge_l, cedge_r, pooled, gmid, near_p, near_g, im_p, im_g,
+    hr, hc, edge, crow, chr_, pooled, pooled_e, gmid, slope_r, slope_e, row_p, pack_p, row_g, pack_g, im_p, im_g,
     a1, gw_in, s_in, s_om, core_in, core_om, half_in, half_om, r1_in, r1_om, r2_in, r2_om, full_in, full_om,
     sem_ps, sem_pr, sem_hs, sem_hr, sem_a, sem_b,
 ):
@@ -119,7 +121,7 @@
     relaid(feat, 0)
     relaid(cot, C)
 
-    gaps = [0, 1, -1, 2, -2, 3, -3, 4, -4]
+    gaps = [0, 2, -2, 4, -4, 1, -1, 3, -3]
 
     def pack(k, dest):
         for s2 in range(0, 4, 2):
@@ -133,58 +135,21 @@
     for k in range(1, 9):
         guarded(has_lat(gaps[k]), lambda k=k: pack(k, pool_s.at[k]))
 
-    lane = lax.broadcasted_iota(jnp.int32, (C, 128), 1)
-
-    def edge_columns(ref, offset, chans, left, right):
+    def edge_columns(ref, offset, chans, to):
         lanes = lax.broadcasted_iota(jnp.int32, (chans, 128), 1)
-        to_l = jnp.zeros((chans, 128), F32)
-        to_r = jnp.zeros((chans, 128), F32)
+        tile = jnp.zeros((chans, 128), F32)
         for r in range(H):
             base = offset + r * W
             first = ref[:, base:base + 128].astype(F32)
             last = ref[:, base + 128:base + 256].astype(F32)
-            to_l = jnp.where(lanes == r + 1, first[:, 0:1], to_l)
-            to_r = jnp.where(lanes == r + 1, last[:, 127:128], to_r)
-        left[...] = to_l.astype(left.dtype)
-        right[...] = to_r.astype(right.dtype)
-
-    edge_columns(fc.at[0:C], 0, C, edge_l.at[FEAT], edge_r.at[FEAT])
-    edge_columns(fc.at[C:2 * C], 0, C, edge_l.at[COT], edge_r.at[COT])
-
-    pl.semaphore_wait(barrier, NLAT * NLON - 1)
-
-    def send_fine(f, ref, offset, rows_at, cols_at, left, right):
-        send(has_lat(-1), ref.at[:, offset:offset + W], rows_at.at[1], sem_hs.at[f, 0], sem_hr.at[f, 1], at(-1, 0))
-        send(has_lat(1), ref.at[:, offset + N - W:offset + N], rows_at.at[0], sem_hs.at[f, 1], sem_hr.at[f, 0], at(1, 0))
-        for d in (0, -1, 1):
-            send(has_lat(d), right, cols_at.at[1 - d], sem_hs.at[f, 3 + d], sem_hr.at[f, 3 - d], at(d, 1))
-            send(has_lat(d), left, cols_at.at[4 - d], sem_hs.at[f, 6 + d], sem_hr.at[f, 6 - d], at(d, -1))
-
-    def expect(cond, ref, sem):
-        if cond is None:
-            arrive(ref, sem)
-            return
-
-        @pl.when(cond)
-        def _():
-            arrive(ref, sem)
-
-        @pl.when(jnp.logical_not(cond))
-        def _():
-            ref[...] = jnp.zeros(ref.shape, ref.dtype)
-
-    def wait_fine(f, rows_at, cols_at):
-        expect(has_lat(-1), rows_at.at[0], sem_hr.at[f, 0])
-        expect(has_lat(1), rows_at.at[1], sem_hr.at[f, 1])
-        for d in (0, -1, 1):
-            expect(has_lat(d), cols_at.at[1 + d], sem_hr.at[f, 3 + d])
-            expect(has_lat(d), cols_at.at[4 + d], sem_hr.at[f, 6 + d])
-
-    for k in range(1, 9):
-        back = gaps.index(-gaps[k])
-        send(has_lat(gaps[k]), pool_s.at[k], pool_r.at[back], sem_ps.at[k], sem_pr.at[back], at(gaps[k], 0))
-    send_fine(FEAT, fc.at[0:C], 0, hr.at[FEAT], hc.at[FEAT], edge_l.at[FEAT], edge_r.at[FEAT])
-    send_fine(COT, fc.at[C:2 * C], 0, hr.at[COT], hc.at[COT], edge_l.at[COT], edge_r.at[COT])
+            tile = jnp.where(lanes == r + 1, first[:, 0:1], tile)
+            tile = jnp.where(lanes == r + 17, last[:, 127:128], tile)
+        if chans < C:
+            tile = jnp.concatenate([tile, jnp.zeros((C - chans, 128), F32)], axis=0)
+        to[...] = tile.T[0:32].astype(BF16)
+
+    edge_columns(fc.at[0:C], 0, C, edge.at[FEAT])
+    edge_columns(fc.at[C:2 * C], 0, C, edge.at[COT])
 
     def make_onehot(j, _):
         m = j // H
@@ -227,22 +192,73 @@
             wt_mid[:, t * C:(t + 1) * C] = turn(w_mid[8 - t])
             wt_in[t // 3, :, (t % 3) * C:(t % 3 + 1) * C] = w_in[8 - t, 0:C, :]
 
-    def left_right(r, cols_at):
+    turn_out()
+
+    pl.semaphore_wait(barrier, NLAT * NLON - 1)
+
+    def send_fine(f, up_row, down_row, rows_at):
+        send(has_lat(-1), up_row, rows_at.at[1], sem_hs.at[f, 0], sem_hr.at[f, 1], at(-1, 0))
+        send(has_lat(1), down_row, rows_at.at[0], sem_hs.at[f, 1], sem_hr.at[f, 0], at(1, 0))
+        for d in (0, -1, 1):
+            left, right = edge.at[f, pl.ds(0, 16)], edge.at[f, pl.ds(16, 16)]
+            send(has_lat(d), right, hc.at[f, pl.ds(16 - 16 * d, 16)], sem_hs.at[f, 3 + d], sem_hr.at[f, 3 - d], at(d, 1))
+            send(has_lat(d), left, hc.at[f, pl.ds(64 - 16 * d, 16)], sem_hs.at[f, 6 + d], sem_hr.at[f, 6 - d], at(d, -1))
+
+    def send_field(f, ref):
+        send_fine(f, ref.at[:, 0:W], ref.at[:, N - W:N], hr.at[f])
+
+    def expect(cond, ref, sem):
+        if cond is None:
+            arrive(ref, sem)
+            return
+
+        @pl.when(cond)
+        def _():
+            arrive(ref, sem)
+
+        @pl.when(jnp.logical_not(cond))
+        def _():
+            ref[...] = jnp.zeros(ref.shape, ref.dtype)
+
+    def wait_fine(f, rows_at):
+        expect(has_lat(-1), rows_at.at[0], sem_hr.at[f, 0])
+        expect(has_lat(1), rows_at.at[1], sem_hr.at[f, 1])
+        for d in (0, -1, 1):
+            expect(has_lat(d), hc.at[f, pl.ds(16 + 16 * d, 16)], sem_hr.at[f, 3 + d])
+            expect(has_lat(d), hc.at[f, pl.ds(64 + 16 * d, 16)], sem_hr.at[f, 6 + d])
+        cols = hc[f, 0:96, :].astype(F32)
+        return jnp.concatenate([cols, jnp.zeros((32, C), F32)], axis=0).T
+
+    def pool_copy(k):
+        back = gaps.index(-gaps[k])
+        return pltpu.make_async_remote_copy(
+            src_ref=pool_s.at[k], dst_ref=pool_r.at[back], send_sem=sem_ps.at[k], recv_sem=sem_pr.at[back],
+            device_id=at(gaps[k], 0), device_id_type=MESH,
+        )
+
+    for k in (5, 6, 7, 8, 1, 2, 3, 4):
+        copy = pool_copy(k)
+        guarded(has_lat(gaps[k]), copy.start)
+        finish.append((has_lat(gaps[k]), copy.wait_send))
+    send_field(FEAT, fc.at[0:C])
+    send_field(COT, fc.at[C:2 * C])
+
+    def left_right(r, cols):
         if r == 0:
-            return cols_at[0].astype(F32)[:, 8:9], cols_at[3].astype(F32)[:, 8:9]
+            return cols[:, 8:9], cols[:, 56:57]
         if r == H + 1:
-            return cols_at[2].astype(F32)[:, 1:2], cols_at[5].astype(F32)[:, 1:2]
-        return cols_at[1].astype(F32)[:, r:r + 1], cols_at[4].astype(F32)[:, r:r + 1]
-
-    def shifted(v, r, cols_at):
+            return cols[:, 33:34], cols[:, 81:82]
+        return cols[:, 16 + r:17 + r], cols[:, 64 + r:65 + r]
+
+    def shifted(v, r, cols):
         chans = v.shape[0]
         at_lane = lax.broadcasted_iota(jnp.int32, (chans, W), 1)
-        first, last = left_right(r, cols_at)
+        first, last = left_right(r, cols)
         before = jnp.where(at_lane == 0, first, pltpu.roll(v, 1, 1))
         after = jnp.where(at_lane == W - 1, last, pltpu.roll(v, W - 1, 1))
         return before, after
 
-    def build(x3, ref, rows_at, cols_at):
+    def build(x3, ref, rows_at, cols):
         for r in range(H + 2):
             if r == 0:
                 v = rows_at[0]
@@ -250,7 +266,7 @@
                 v = rows_at[1]
             else:
                 v = ref[:, (r - 1) * W:r * W]
-            before, after = shifted(v.astype(F32), r, cols_at)
+            before, after = shifted(v.astype(F32), r, cols)
             x3[0:C, r * W:(r + 1) * W] = before.astype(BF16)
             x3[C:2 * C, r * W:(r + 1) * W] = v
             x3[2 * C:3 * C, r * W:(r + 1) * W] = after.astype(BF16)
@@ -275,12 +291,9 @@
 
         return use
 
-    wait_fine(FEAT, hr.at[FEAT], hc.at[FEAT])
-    build(x3f, fc.at[0:C], hr.at[FEAT], hc.at[FEAT])
+    build(x3f, fc.at[0:C], hr.at[FEAT], wait_fine(FEAT, hr.at[FEAT]))
     conv(wf, x3f, put(hidden))
-    turn_out()
-    wait_fine(COT, hr.at[COT], hc.at[COT])
-    build(x3c, fc.at[C:2 * C], hr.at[COT], hc.at[COT])
+    build(x3c, fc.at[C:2 * C], hr.at[COT], wait_fine(COT, hr.at[COT]))
     conv(wt_out, x3c, put(gmerged))
 
     def halves(v):
@@ -293,7 +306,8 @@
     acc[...] = jnp.zeros(acc.shape, F32)
 
     def interp(k, _):
-        gap = jnp.where(lax.rem(k, 2) == 1, (k + 1) // 2, -(k // 2))
+        size = lax.rem(2 * ((k + 1) // 2), 5)
+        gap = jnp.where(lax.rem(k, 2) == 1, size, -size)
         owner = lat + gap
 
         @pl.when(jnp.logical_and(owner >= 0, owner < NLAT))
@@ -315,17 +329,20 @@
 
     blended = acc[:, 0:N] + acc[:, N:2 * N]
     condf[:, W:W + N] = blended.astype(BF16).astype(F32)
-    edge_columns(condf, W, CC, cedge_l, cedge_r)
-    send_fine(COND, condf, W, chr_, chc, cedge_l, cedge_r)
-    wait_fine(COND, chr_, chc)
+    edge_columns(condf, W, CC, edge.at[COND])
+    for i, start in enumerate((W, N)):
+        row = jnp.concatenate([condf[:, start:start + W], jnp.zeros((8, W), F32)], axis=0)
+        crow[i] = row.astype(BF16)
+    send_fine(COND, crow.at[0], crow.at[1], chr_)
+    cond_cols = wait_fine(COND, chr_)[0:CC]
     for r in range(H + 2):
         if r == 0:
-            v = chr_[0]
+            v = chr_[0].astype(F32)[0:CC]
         elif r == H + 1:
-            v = chr_[1]
+            v = chr_[1].astype(F32)[0:CC]
         else:
             v = condf[:, r * W:(r + 1) * W]
-        before, after = shifted(v, r, chc)
+        before, after = shifted(v, r, cond_cols)
         stacked = jnp.concatenate([before, v, after, jnp.zeros((8, W), F32)], axis=0)
         x3cond[:, r * W:(r + 1) * W] = stacked.astype(BF16)
 
@@ -340,6 +357,9 @@
     to_first = jnp.where(other == chan // (C // G), 1.0, 0.0)
     to_second = jnp.where(other == G + chan // (C // G), 1.0, 0.0)
     me = lat * NLON + lon
+
+    def to_row(col):
+        return jnp.sum(jnp.where(eye, col, 0.0), axis=0, keepdims=True)
 
     def to_col(row):
         return jnp.sum(jnp.where(eye, row, 0.0), axis=1, keepdims=True)
@@ -394,36 +414,63 @@
 
     lax.fori_loop(0, H, activate, 0)
 
-    def send_coarse(f, ref, near):
-        for i, (dlat, dlon) in enumerate(AROUND):
-            send(has_lat(dlat), ref, near.at[7 - i], sem_hs.at[f, i], sem_hr.at[f, 7 - i], at(dlat, dlon))
-
-    def wait_coarse(f, near):
-        for i, (dlat, dlon) in enumerate(AROUND):
-            expect(has_lat(dlat), near.at[i], sem_hr.at[f, i])
-
-    def build_coarse(im, ref, near):
-        def column(up_, mid_, down_):
-            u, m, d = up_.astype(F32), mid_.astype(F32), down_.astype(F32)
-            over = jnp.where(lane < 64, pltpu.roll(u, 64, 1), pltpu.roll(m, 64, 1))
-            under = jnp.where(lane < 64, pltpu.roll(m, 64, 1), pltpu.roll(d, 64, 1))
-            return over, m, under
-
-        lefts = column(near[0], near[3], near[5])
-        mids = column(near[1], ref[...], near[6])
-        rights = column(near[2], near[4], near[7])
-        for a in range(3):
-            before = jnp.where(lane % 64 == 0, pltpu.roll(lefts[a], 65, 1), pltpu.roll(mids[a], 1, 1))
-            after = jnp.where(lane % 64 == 63, pltpu.roll(rights[a], 63, 1), pltpu.roll(mids[a], 127, 1))
-            im[(3 * a) * C:(3 * a + 1) * C] = before.astype(BF16)
-            im[(3 * a + 1) * C:(3 * a + 2) * C] = mids[a].astype(BF16)
-            im[(3 * a + 2) * C:(3 * a + 3) * C] = after.astype(BF16)
-
-    pooled[...] = (dot_nt(act[...], up[...]) * (1.0 / 16.0)).astype(BF16)
-    send_coarse(POOL, pooled, near_p)
-    wait_coarse(POOL, near_p)
-    build_coarse(im_p, pooled, near_p)
-    hidden_mid = dot(wm[...], im_p[...])
+    def send_coarse(f, rows, near, mine, packs):
+        half = rows.shape[0] // 2
+        send(has_lat(-1), rows.at[pl.ds(0, half)], near.at[1], sem_hs.at[f, 0], sem_hr.at[f, 1], at(-1, 0))
+        send(has_lat(1), rows.at[pl.ds(half, half)], near.at[0], sem_hs.at[f, 1], sem_hr.at[f, 0], at(1, 0))
+        for d in (0, -1, 1):
+            send(has_lat(d), mine, packs.at[1 - d], sem_hs.at[f, 3 + d], sem_hr.at[f, 3 - d], at(d, 1))
+            send(has_lat(d), mine, packs.at[4 - d], sem_hs.at[f, 6 + d], sem_hr.at[f, 6 - d], at(d, -1))
+
+    def wait_coarse(f, near, packs):
+        expect(has_lat(-1), near.at[0], sem_hr.at[f, 0])
+        expect(has_lat(1), near.at[1], sem_hr.at[f, 1])
+        for d in (0, -1, 1):
+            expect(has_lat(d), packs.at[1 + d], sem_hr.at[f, 3 + d])
+            expect(has_lat(d), packs.at[4 + d], sem_hr.at[f, 6 + d])
+
+    sub16 = lax.broadcasted_iota(jnp.int32, (16, C), 0)
+
+    def corner_rows(v, first, base):
+        for i, n in enumerate((0, 64, 63, 127)):
+            base = jnp.where(sub16 == first + i, v[n:n + 1], base)
+        return base
+
+    def around(own, near, packs, part, first):
+        size = 64
+        above = near[0].astype(F32)[part * size:(part + 1) * size]
+        below = near[1].astype(F32)[part * size:(part + 1) * size]
+        full = jnp.concatenate([above, own, below], axis=0)
+        ends = [packs[i].astype(F32) for i in range(6)]
+
+        def row(i, n):
+            return ends[i][first + n:first + n + 1]
+
+        lefts = [row(0, 3), row(1, 2), row(1, 3), row(2, 2)]
+        rights = [row(3, 1), row(4, 0), row(4, 1), row(5, 0)]
+        return full, lefts, rights
+
+    cells = lax.broadcasted_iota(jnp.int32, (2 * C, C), 0)
+
+    def build_coarse(im, full, lefts, rights):
+        before = pltpu.roll(full, 1, 0)
+        after = pltpu.roll(full, 2 * C - 1, 0)
+        for k in range(4):
+            before = jnp.where(cells == 64 * k, lefts[k], before)
+            after = jnp.where(cells == 64 * k + 63, rights[k], after)
+        for b, v in enumerate((before, full, after)):
+            v = v.astype(BF16)
+            for a in range(3):
+                im[:, (3 * a + b) * C:(3 * a + b + 1) * C] = v[a * 64:a * 64 + C]
+
+    own = (dot_nt(up[...], act[...]) * (1.0 / 16.0)).astype(BF16)
+    pooled[...] = own
+    own = own.astype(F32)
+    pooled_e[...] = corner_rows(own, 0, jnp.zeros((16, C), F32)).astype(BF16)
+    send_coarse(POOL, pooled, row_p, pooled_e, pack_p)
+    wait_coarse(POOL, row_p, pack_p)
+    build_coarse(im_p, *around(own, row_p, pack_p, 0, 0))
+    hidden_mid = dot_nt(wm[...], im_p[...])
     sums, squares = all_sum(1, hidden_mid, hidden_mid * hidden_mid)
     avg_mid, inv_mid = norm_terms(sums, squares, MEMBERS // 16)
     normed_mid = (hidden_mid - avg_mid) * inv_mid
@@ -431,25 +478,43 @@
     sig = sigmoid(affine_mid)
     act_mid = (affine_mid * sig).astype(BF16)
     slope_mid = gsmall * sig * (1.0 + affine_mid * (1.0 - sig)) * g2
-
-    def send_merged():
+    slope_t = slope_mid.T
+    normed_t = normed_mid.T
+
+    def send_slopes():
+        for i, n in enumerate((0, 64)):
+            slope_r[i * C:i * C + 64] = slope_t[n:n + 64].astype(BF16)
+            slope_r[i * C + 64:(i + 1) * C] = normed_t[n:n + 64].astype(BF16)
+        ends = corner_rows(slope_t, 0, jnp.zeros((16, C), F32))
+        slope_e[...] = corner_rows(normed_t, 4, ends).astype(BF16)
+        send_coarse(GMID, slope_r, row_g, slope_e, pack_g)
         for r in range(H):
             where = slice(r * W, (r + 1) * W)
             merged[:, where] = (act[:, where].astype(F32) + dot(act_mid, up[:, where])).astype(BF16)
-        edge_columns(merged, 0, C, edge_l.at[MERG], edge_r.at[MERG])
-        send_fine(MERG, merged, 0, hr.at[MERG], hc.at[MERG], edge_l.at[MERG], edge_r.at[MERG])
-
-    sum_e, sum_en = all_sum(2, slope_mid, slope_mid * normed_mid, send_merged)
+        edge_columns(merged, 0, C, edge.at[MERG])
+        send_field(MERG, merged)
+
+    sum_e, sum_en = all_sum(2, slope_mid, slope_mid * normed_mid, send_slopes)
     mean_e = sum_e / (MEMBERS // 16)
     mean_en = sum_en / (MEMBERS // 16)
     gmid[...] = ((slope_mid - mean_e - normed_mid * mean_en) * inv_mid).astype(BF16)
-    send_coarse(GMID, gmid, near_g)
-    g_mid_w = dot_nt(gmid[...], im_p[...])
-    for t in range(9):
-        s_om[t * C:(t + 1) * C] = g_mid_w[:, t * C:(t + 1) * C].astype(BF16)
-    wait_coarse(GMID, near_g)
-    build_coarse(im_g, gmid, near_g)
-    gpooled = dot(wt_mid[...], im_g[...]) * (1.0 / 16.0)
+    wait_coarse(GMID, row_g, pack_g)
+    row_e, row_en, row_inv = to_row(mean_e), to_row(mean_en), to_row(inv_mid)
+    inside = [jnp.where(lat > 0, 1.0, 0.0), 1.0, 1.0, jnp.where(lat < NLAT - 1, 1.0, 0.0)]
+
+    def settled(e, normed):
+        return (e - row_e - normed * row_en) * row_inv
+
+    e_all, e_left, e_right = around(slope_t, row_g, pack_g, 0, 0)
+    n_all, n_left, n_right = around(normed_t, row_g, pack_g, 1, 4)
+    valid = jnp.where(cells < 64, inside[0], jnp.where(cells < 192, 1.0, inside[3]))
+    build_coarse(
+        im_g,
+        settled(e_all, n_all) * valid,
+        [settled(e_left[k], n_left[k]) * inside[k] for k in range(4)],
+        [settled(e_right[k], n_right[k]) * inside[k] for k in range(4)],
+    )
+    gpooled = dot_nt(wt_mid[...], im_g[...]) * (1.0 / 16.0)
     high, low = halves(gpooled)
 
     def slopes(j, carry):
@@ -529,23 +594,25 @@
         hand(k, 4, full.at[core], full.at[core], partner)
         finish.append((None, lambda: arrive(full.at[core], sem_b.at[k, 8])))
 
-    def complete(k, result):
-        full = jobs[k][6]
+    def complete(k, base):
+        rows, full = jobs[k][0], jobs[k][6]
         arrive(full.at[1 - core], sem_b.at[k, 9])
-        result[...] = full[...]
+        res[base:base + 16 * rows] = full[...].reshape(16 * rows, C)
 
     def beside_slopes():
-        wait_fine(MERG, hr.at[MERG], hc.at[MERG])
-        build(x3m, merged, hr.at[MERG], hc.at[MERG])
+        build(x3m, merged, hr.at[MERG], wait_fine(MERG, hr.at[MERG]))
         for a in range(3):
             part = dot_nt(fc[C:2 * C], x3m[:, a * W:a * W + N])
             for b in range(3):
                 t = 9 + 3 * a + b
                 s_om[t * C:(t + 1) * C] = part[:, b * C:(b + 1) * C].astype(BF16)
+        g_mid_w = dot(gmid[...], im_p[...])
+        for t in range(9):
+            s_om[t * C:(t + 1) * C] = g_mid_w[:, t * C:(t + 1) * C].astype(BF16)
         cores(0)
-        scatter(0)
 
     sum_e, sum_en = all_sum(3, s, q, beside_slopes)
+    scatter(0)
     mean_e = sum_e / MEMBERS
     mean_en = sum_en / MEMBERS
 
@@ -557,8 +624,6 @@
 
     lax.fori_loop(0, H, finish_in, 0)
 
-    edge_columns(gin, 0, C, edge_l.at[GIN], edge_r.at[GIN])
-    send_fine(GIN, gin, 0, hr.at[GIN], hc.at[GIN], edge_l.at[GIN], edge_r.at[GIN])
     taps = C + CC
     for a in range(3):
         part = dot_nt(x3f[:, a * W:a * W + N], gin[...])
@@ -570,29 +635,51 @@
     gw_in[9 * taps:] = jnp.zeros((16 * ROWS_IN - 9 * taps, C), F32)
     s_in[...] = gw_in[...].astype(BF16)
     cores(1)
+    edge_columns(gin, 0, C, edge.at[GIN])
+    send_field(GIN, gin)
+    scatter(1)
+
+    def put_rows(base, where, v):
+        for i in range(STEP // 128):
+            res[pl.ds(pl.multiple_of(base + where.start + i * 128, 128), C)] = v[:, i * 128:(i + 1) * 128]
+
+    def put_out(where, v):
+        put_rows(0, where, (fc[0:C, where].astype(F32) + v).astype(BF16))
+
+    conv(wo, x3m, put_out)
     middle(0)
-    scatter(1)
-
-    def put_out(where, v):
-        out[:, where] = (fc[0:C, where].astype(F32) + v).astype(BF16)
-
-    conv(wo, x3m, put_out)
+    middle(1)
+    build(x3g, gin, hr.at[GIN], wait_fine(GIN, hr.at[GIN]))
+
+    def put_feat(where, v):
+        put_rows(2 * H * C, where, (fc[C:2 * C, where].astype(F32) + v).astype(BF16))
+
     gather(0)
-    middle(1)
-    wait_fine(GIN, hr.at[GIN], hc.at[GIN])
-    build(x3g, gin, hr.at[GIN], hc.at[GIN])
-
-    def put_feat(where, v):
-        gfeat[:, where] = (fc[C:2 * C, where].astype(F32) + v).astype(BF16)
-
     conv(wt_in, x3g, put_feat)
     gather(1)
     exchange(0)
-    complete(0, g_om)
+    complete(0, AT_OM)
     exchange(1)
-    complete(1, g_in)
+    complete(1, AT_IN)
     for cond, wait in finish:
         guarded(cond, wait)
+
+
+def results(res_h, field, features, grad_in, grad_mid, grad_out, res, relay, sem):
+    move = pltpu.make_async_copy(res_h, res, sem)
+    move.start()
+    move.wait()
+    for base, dest in ((0, field), (2 * H * C, features)):
+        for side in range(2):
+            for r in range(H):
+                start = base + (2 * r + side) * C
+                relay[pl.ds(r, C, stride=H), :] = res[start:start + C].astype(F32)
+            dest[:, :, side * 128:(side + 1) * 128] = relay[...].reshape(C, H, 128).astype(BF16)
+    for t in range(9):
+        rows = slice(AT_IN + t * (C + CC), AT_IN + (t + 1) * (C + CC))
+        grad_in[t] = res[rows].astype(F32) * FACTOR
+        grad_mid[t] = res[AT_OM + t * C:AT_OM + (t + 1) * C].astype(F32) * FACTOR
+        grad_out[t] = res[AT_OM + (9 + t) * C:AT_OM + (10 + t) * C].astype(F32) * FACTOR
 
 
 def local(
@@ -601,6 +688,7 @@
 ):
     vmem = pl.BlockSpec(memory_space=pltpu.VMEM)
     smem = pl.BlockSpec(memory_space=pltpu.SMEM)
+    hbm = pl.BlockSpec(memory_space=pltpu.HBM)
     V = pltpu.VMEM
     scratch = [
         V((2 * C, N), BF16), V((2 * C * H, 128), F32),
@@ -611,10 +699,10 @@
         V((3 * C, NP), BF16), V((3 * C, NP), BF16), V((3 * C, NP), BF16), V((3 * C, NP), BF16), V((C, NP), BF16),
         V((3, C, 3 * C), BF16), V((3, C, C), BF16), V((3, C, 3 * C), BF16), V((C, 9 * C), BF16),
         V((3, C, 3 * C), BF16), V((C, 9 * C), BF16), V((3, C, 3 * C), BF16),
-        V((7, 2, C, W), BF16), V((7, 6, C, 128), BF16), V((7, C, 128), BF16), V((7, C, 128), BF16),
-        V((2, CC, W), F32), V((6, CC, 128), F32), V((CC, 128), F32), V((CC, 128), F32),
-        V((C, 128), BF16), V((C, 128), BF16), V((8, C, 128), BF16), V((8, C, 128), BF16),
-        V((9 * C, 128), BF16), V((9 * C, 128), BF16),
+        V((7, 2, C, W), BF16), V((7, C, C), BF16), V((7, 32, C), BF16), V((2, 48, W), BF16), V((2, 48, W), BF16),
+        V((C, C), BF16), V((16, C), BF16), V((C, C), BF16), V((2 * C, C), BF16), V((16, C), BF16),
+        V((2, 64, C), BF16), V((6, 16, C), BF16), V((2, C, C), BF16), V((6, 16, C), BF16),
+        V((C, 9 * C), BF16), V((C, 9 * C), BF16),
         V((4, NLAT * NLON, C), F32), V((16 * ROWS_IN, C), F32),
         V((16 * ROWS_IN, C), BF16), V((16 * ROWS_OM, C), BF16), V((8 * ROWS_IN, C), BF16), V((8 * ROWS_OM, C), BF16),
         V((8 * ROWS_IN, C), BF16), V((8 * ROWS_OM, C), BF16), V((8, ROWS_IN, C), BF16), V((8, ROWS_OM, C), BF16),
@@ -623,14 +711,11 @@
         pltpu.SemaphoreType.DMA((7, 8)), pltpu.SemaphoreType.DMA((7, 8)),
         pltpu.SemaphoreType.DMA((4, 2)), pltpu.SemaphoreType.DMA((2, 10)),
     ]
-    out, gfeat, g_in, g_om = pl.pallas_call(
+    res = pl.pallas_call(
         kernel,
-        out_shape=(
-            jax.ShapeDtypeStruct((C, N), BF16), jax.ShapeDtypeStruct((C, N), BF16),
-            jax.ShapeDtypeStruct((2, 8, ROWS_IN, C), BF16), jax.ShapeDtypeStruct((2, 8, ROWS_OM, C), BF16),
-        ),
+        out_shape=jax.ShapeDtypeStruct((ROWS, C), BF16),
         in_specs=[vmem, vmem, vmem, smem] + [vmem] * 9,
-        out_specs=(vmem,) * 4,
+        out_specs=vmem,
         scratch_shapes=scratch,
         compiler_params=pltpu.CompilerParams(
             collective_id=0, has_side_effects=True, vmem_limit_bytes=56 * 1024 * 1024
@@ -639,13 +724,19 @@
         features, cotangent, coarse_blocks, send_table, interp_src, interp_wt, jnp.swapaxes(weight_in, 1, 2), weight_mid, weight_out,
         gain_in.reshape(1, C), bias_in.reshape(1, C), gain_mid.reshape(1, C), bias_mid.reshape(1, C),
     )
-    shape = features.shape
-    grad_in = g_in.reshape(16 * ROWS_IN, C)[:9 * (C + CC)].reshape(9, C + CC, C).astype(F32) * FACTOR
-    grad_in = jnp.swapaxes(grad_in, 1, 2)
-    taps = g_om.reshape(18, C, C)
-    grad_mid = taps[:9].astype(F32) * FACTOR
-    grad_out = taps[9:].astype(F32) * FACTOR
-    return out.reshape(shape), gfeat.reshape(shape), grad_in, grad_mid, grad_out
+    field, grad_features, grad_in, grad_mid, grad_out = pl.pallas_call(
+        results,
+        out_shape=(
+            jax.ShapeDtypeStruct((C, H, W), BF16), jax.ShapeDtypeStruct((C, H, W), BF16),
+            jax.ShapeDtypeStruct((9, C + CC, C), F32),
+            jax.ShapeDtypeStruct((9, C, C), F32), jax.ShapeDtypeStruct((9, C, C), F32),
+        ),
+        in_specs=[hbm],
+        out_specs=(vmem,) * 5,
+        scratch_shapes=[V((ROWS, C), BF16), V((C * H, 128), F32), pltpu.SemaphoreType.DMA],
+        compiler_params=pltpu.CompilerParams(vmem_limit_bytes=60 * 1024 * 1024),
+    )(res)
+    return field, grad_features, jnp.swapaxes(grad_in, 1, 2), grad_mid, grad_out
 
 
 def solution(mesh):

time: 131 us -> 114 us (0.87)
  Pallas kernels: 125 us -> 113 us
  other arithmetic: 3.12 us -> 0 us
  local copies, waits for them, and re-layouts: 2.33 us -> 0 us
    pallas_call x1 -> x2, Pallas kernels: 125 us -> 113 us  [the longest x1 109 us: local(): pl.pallas_call(kernel, out_shape=jax.ShapeDtypeStruct((ROWS, C), BF16), i...]
    mul x2 -> x0, other arithmetic: 3.12 us -> none  [the longest x1 2.19 us: local(): grad_out = taps[9:].astype(F32) * FACTOR]
    unnamed x8 -> x0, local copies, waits for them, and re-layouts: 2.33 us -> none
where the time goes in v2:
time: 114 us; the launch traced here: 113 us
  Pallas kernels  113 us (99%)
    pallas_call x1, Pallas kernels, local(): pl.pallas_call(kernel, out_shape=jax.ShapeDtypeStruct((ROWS, C), BF16), i...  109 us
    pallas_call x1, Pallas kernels, local(): pl.pallas_call(results, out_shape=(jax.ShapeDtypeStruct((C, H, W), BF16),...  3.76 us

profile of v2, /device:TPU:1, one launch (start us, length us, event | category | flops | bytes accessed | tf_op | source)
XLA Modules:
  0.0 113.4 jit_solution(10755558358012406874)
XLA Ops:
  0.6 108.8 %shard_map.164.res_h = bf16[7936,128]{1,0:T(8,128)(2,1)} custom-call(bf16[128,8,256]{2,1,0:T(8,128)(2,1)} %feat.1, bf16[128,8,256]{2,1,0:T(8,128)(2,1)} %cot.1, bf16[1,16,40,256]{3,2,1,0:T(8,128)(2,1)} %blocks.1, s32[1,8,8,8]{3,2,1,0:T(8,128)} %table.1, s32[2,8,256]{2,1,0:T(8,128)} %src.1, f32[2,8,256]{2,1,0:T(8,128)} %wt.1, bf16[9,168,128]{2,1,0:T(8,128)(2,1)} %bitcast.6, ...), custom_call_target="tpu_custom_call" | custom-call | tf_op jit(solution)/shard_map/pallas_call | solution.py:714
  109.5 3.8 %shard_map.165 = (bf16[128,8,256]{2,1,0:T(8,128)(2,1)}, bf16[128,8,256]{2,1,0:T(8,128)(2,1)}, f32[9,168,128]{2,1,0:T(8,128)}, f32[9,128,128]{2,1,0:T(8,128)}, f32[9,128,128]{2,1,0:T(8,128)}) custom-call(bf16[7936,128]{1,0:T(8,128)(2,1)} %shard_map.164.res_h), custom_call_target="tpu_custom_call" | custom-call | tf_op jit(solution)/shard_map/pallas_call | solution.py:727

commit v3 on v2

--- a/solution.py
+++ b/solution.py
@@ -22,7 +22,7 @@
 EPS = 1e-05
 ROWS_IN = 96
 ROWS_OM = 144
-AT_OM = 4 * H * C
+AT_OM = 0
 AT_IN = AT_OM + 16 * ROWS_OM
 ROWS = AT_IN + 16 * ROWS_IN
 F32 = jnp.float32
@@ -50,11 +50,11 @@
 
 def kernel(
     feat, cot, blocks, table, src, wt, w_in, w_mid, w_out, gain_in, bias_in, gain_mid, bias_mid,
-    res,
+    fields, res,
     fc, relay, pool_s, pool_r, onehot, fid, fwt, acc, condf, hidden, gmerged, slope, act, merged, gin, up,
     x3f, x3c, x3m, x3g, x3cond, wf, wc, wo, wm, wt_out, wt_mid, wt_in,
     hr, hc, edge, crow, chr_, pooled, pooled_e, gmid, slope_r, slope_e, row_p, pack_p, row_g, pack_g, im_p, im_g,
-    a1, gw_in, s_in, s_om, core_in, core_om, half_in, half_om, r1_in, r1_om, r2_in, r2_om, full_in, full_om,
+    gsmall, a1, gw_in, s_in, s_om, core_in, core_om, half_in, half_om, r1_in, r1_om, r2_in, r2_om, full_in, full_om,
     sem_ps, sem_pr, sem_hs, sem_hr, sem_a, sem_b,
 ):
     lon = lax.axis_index("lon")
@@ -149,7 +149,6 @@
         to[...] = tile.T[0:32].astype(BF16)
 
     edge_columns(fc.at[0:C], 0, C, edge.at[FEAT])
-    edge_columns(fc.at[C:2 * C], 0, C, edge.at[COT])
 
     def make_onehot(j, _):
         m = j // H
@@ -241,7 +240,6 @@
         guarded(has_lat(gaps[k]), copy.start)
         finish.append((has_lat(gaps[k]), copy.wait_send))
     send_field(FEAT, fc.at[0:C])
-    send_field(COT, fc.at[C:2 * C])
 
     def left_right(r, cols):
         if r == 0:
@@ -293,15 +291,9 @@
 
     build(x3f, fc.at[0:C], hr.at[FEAT], wait_fine(FEAT, hr.at[FEAT]))
     conv(wf, x3f, put(hidden))
-    build(x3c, fc.at[C:2 * C], hr.at[COT], wait_fine(COT, hr.at[COT]))
-    conv(wt_out, x3c, put(gmerged))
-
     def halves(v):
         high = v.astype(BF16)
         return high, (v - high.astype(F32)).astype(BF16)
-
-    high, low = halves(gmerged[...])
-    gsmall = dot_nt(high, up[...]) + dot_nt(low, up[...])
 
     acc[...] = jnp.zeros(acc.shape, F32)
 
@@ -399,7 +391,12 @@
         v = hidden[:, j * 128:(j + 1) * 128]
         s = s + v
         q = q + v * v
-    sums, squares = all_sum(0, s, q, turn_rest)
+    def beside_first():
+        edge_columns(fc.at[C:2 * C], 0, C, edge.at[COT])
+        send_field(COT, fc.at[C:2 * C])
+        turn_rest()
+
+    sums, squares = all_sum(0, s, q, beside_first)
     avg_in, inv_in = norm_terms(sums, squares, MEMBERS)
     g1 = to_col(gain_in[...])
     b1 = to_col(bias_in[...])
@@ -471,13 +468,20 @@
     wait_coarse(POOL, row_p, pack_p)
     build_coarse(im_p, *around(own, row_p, pack_p, 0, 0))
     hidden_mid = dot_nt(wm[...], im_p[...])
-    sums, squares = all_sum(1, hidden_mid, hidden_mid * hidden_mid)
+
+    def beside_second():
+        build(x3c, fc.at[C:2 * C], hr.at[COT], wait_fine(COT, hr.at[COT]))
+        conv(wt_out, x3c, put(gmerged))
+        high, low = halves(gmerged[...])
+        gsmall[...] = dot_nt(high, up[...]) + dot_nt(low, up[...])
+
+    sums, squares = all_sum(1, hidden_mid, hidden_mid * hidden_mid, beside_second)
     avg_mid, inv_mid = norm_terms(sums, squares, MEMBERS // 16)
     normed_mid = (hidden_mid - avg_mid) * inv_mid
     affine_mid = g2 * normed_mid + b2
     sig = sigmoid(affine_mid)
     act_mid = (affine_mid * sig).astype(BF16)
-    slope_mid = gsmall * sig * (1.0 + affine_mid * (1.0 - sig)) * g2
+    slope_mid = gsmall[...] * sig * (1.0 + affine_mid * (1.0 - sig)) * g2
     slope_t = slope_mid.T
     normed_t = normed_mid.T
 
@@ -639,23 +643,31 @@
     send_field(GIN, gin)
     scatter(1)
 
-    def put_rows(base, where, v):
+    def put_relaid(where, v):
         for i in range(STEP // 128):
-            res[pl.ds(pl.multiple_of(base + where.start + i * 128, 128), C)] = v[:, i * 128:(i + 1) * 128]
+            first = (i % 2) * C * H + where.start // W + i // 2
+            relay[pl.ds(first, C, stride=H), :] = v[:, i * 128:(i + 1) * 128]
+
+    def put_field(base):
+        for side in range(2):
+            cells = relay[side * C * H:(side + 1) * C * H].reshape(C, H, 128)
+            fields[base:base + C, :, side * 128:(side + 1) * 128] = cells.astype(BF16)
 
     def put_out(where, v):
-        put_rows(0, where, (fc[0:C, where].astype(F32) + v).astype(BF16))
+        put_relaid(where, fc[0:C, where].astype(F32) + v)
 
     conv(wo, x3m, put_out)
+    put_field(0)
     middle(0)
     middle(1)
     build(x3g, gin, hr.at[GIN], wait_fine(GIN, hr.at[GIN]))
 
     def put_feat(where, v):
-        put_rows(2 * H * C, where, (fc[C:2 * C, where].astype(F32) + v).astype(BF16))
+        put_relaid(where, fc[C:2 * C, where].astype(F32) + v)
 
     gather(0)
     conv(wt_in, x3g, put_feat)
+    put_field(C)
     gather(1)
     exchange(0)
     complete(0, AT_OM)
@@ -665,21 +677,21 @@
         guarded(cond, wait)
 
 
-def results(res_h, field, features, grad_in, grad_mid, grad_out, res, relay, sem):
-    move = pltpu.make_async_copy(res_h, res, sem)
-    move.start()
-    move.wait()
-    for base, dest in ((0, field), (2 * H * C, features)):
-        for side in range(2):
-            for r in range(H):
-                start = base + (2 * r + side) * C
-                relay[pl.ds(r, C, stride=H), :] = res[start:start + C].astype(F32)
-            dest[:, :, side * 128:(side + 1) * 128] = relay[...].reshape(C, H, 128).astype(BF16)
+def results(fields, res_h, field, features, grad_in, grad_mid, grad_out, res, sem):
+    moves = [
+        pltpu.make_async_copy(a, b, sem.at[i])
+        for i, (a, b) in enumerate(((res_h, res), (fields.at[0:C], field), (fields.at[C:2 * C], features)))
+    ]
+    for move in moves:
+        move.start()
+    moves[0].wait()
     for t in range(9):
         rows = slice(AT_IN + t * (C + CC), AT_IN + (t + 1) * (C + CC))
         grad_in[t] = res[rows].astype(F32) * FACTOR
         grad_mid[t] = res[AT_OM + t * C:AT_OM + (t + 1) * C].astype(F32) * FACTOR
         grad_out[t] = res[AT_OM + (9 + t) * C:AT_OM + (10 + t) * C].astype(F32) * FACTOR
+    for move in moves[1:]:
+        move.wait()
 
 
 def local(
@@ -703,7 +715,7 @@
         V((C, C), BF16), V((16, C), BF16), V((C, C), BF16), V((2 * C, C), BF16), V((16, C), BF16),
         V((2, 64, C), BF16), V((6, 16, C), BF16), V((2, C, C), BF16), V((6, 16, C), BF16),
         V((C, 9 * C), BF16), V((C, 9 * C), BF16),
-        V((4, NLAT * NLON, C), F32), V((16 * ROWS_IN, C), F32),
+        V((C, C), F32), V((4, NLAT * NLON, C), F32), V((16 * ROWS_IN, C), F32),
         V((16 * ROWS_IN, C), BF16), V((16 * ROWS_OM, C), BF16), V((8 * ROWS_IN, C), BF16), V((8 * ROWS_OM, C), BF16),
         V((8 * ROWS_IN, C), BF16), V((8 * ROWS_OM, C), BF16), V((8, ROWS_IN, C), BF16), V((8, ROWS_OM, C), BF16),
         V((8, ROWS_IN, C), BF16), V((8, ROWS_OM, C), BF16), V((2, 8, ROWS_IN, C), BF16), V((2, 8, ROWS_OM, C), BF16),
@@ -711,11 +723,11 @@
         pltpu.SemaphoreType.DMA((7, 8)), pltpu.SemaphoreType.DMA((7, 8)),
         pltpu.SemaphoreType.DMA((4, 2)), pltpu.SemaphoreType.DMA((2, 10)),
     ]
-    res = pl.pallas_call(
+    fields, res = pl.pallas_call(
         kernel,
-        out_shape=jax.ShapeDtypeStruct((ROWS, C), BF16),
+        out_shape=(jax.ShapeDtypeStruct((2 * C, H, W), BF16), jax.ShapeDtypeStruct((ROWS, C), BF16)),
         in_specs=[vmem, vmem, vmem, smem] + [vmem] * 9,
-        out_specs=vmem,
+        out_specs=(vmem, vmem),
         scratch_shapes=scratch,
         compiler_params=pltpu.CompilerParams(
             collective_id=0, has_side_effects=True, vmem_limit_bytes=56 * 1024 * 1024
@@ -731,11 +743,11 @@
             jax.ShapeDtypeStruct((9, C + CC, C), F32),
             jax.ShapeDtypeStruct((9, C, C), F32), jax.ShapeDtypeStruct((9, C, C), F32),
         ),
-        in_specs=[hbm],
+        in_specs=[hbm, hbm],
         out_specs=(vmem,) * 5,
-        scratch_shapes=[V((ROWS, C), BF16), V((C * H, 128), F32), pltpu.SemaphoreType.DMA],
+        scratch_shapes=[V((ROWS, C), BF16), pltpu.SemaphoreType.DMA((3,))],
         compiler_params=pltpu.CompilerParams(vmem_limit_bytes=60 * 1024 * 1024),
-    )(res)
+    )(fields, res)
     return field, grad_features, jnp.swapaxes(grad_in, 1, 2), grad_mid, grad_out
 
 

time: 114 us -> 110 us (0.965)
  Pallas kernels: 113 us -> 109 us
    pallas_call x1, Pallas kernels: 109 us -> 106 us  [local(): pl.pallas_call(kernel, out_shape=(jax.ShapeDtypeStruct((2 * C, H, W), BF1...]
where the time goes in v3:
time: 110 us
  Pallas kernels  109 us (99%)
    pallas_call x1, Pallas kernels, local(): pl.pallas_call(kernel, out_shape=(jax.ShapeDtypeStruct((2 * C, H, W), BF1...  106 us
    pallas_call x1, Pallas kernels, local(): pl.pallas_call(results, out_shape=(jax.ShapeDtypeStruct((C, H, W), BF16),...  3.13 us

profile of v3, /device:TPU:1, one launch (start us, length us, event | category | flops | bytes accessed | tf_op | source)
XLA Modules:
  0.0 109.7 jit_solution(6387815098798409964)
XLA Ops:
  0.6 105.8 %shard_map.164 = (bf16[256,8,256]{2,1,0:T(8,128)(2,1)}, bf16[3840,128]{1,0:T(8,128)(2,1)}) custom-call(bf16[128,8,256]{2,1,0:T(8,128)(2,1)} %feat.1, bf16[128,8,256]{2,1,0:T(8,128)(2,1)} %cot.1, bf16[1,16,40,256]{3,2,1,0:T(8,128)(2,1)} %blocks.1, s32[1,8,8,8]{3,2,1,0:T(8,128)} %table.1, s32[2,8,256]{2,1,0:T(8,128)} %src.1, f32[2,8,256]{2,1,0:T(8,128)} %wt.1, ...), custom_call_target="tpu_custom_call" | custom-call | tf_op jit(solution)/shard_map/pallas_call | solution.py:726
  106.4 3.1 %shard_map.165 = (bf16[128,8,256]{2,1,0:T(8,128)(2,1)}, bf16[128,8,256]{2,1,0:T(8,128)(2,1)}, f32[9,168,128]{2,1,0:T(8,128)}, f32[9,128,128]{2,1,0:T(8,128)}, f32[9,128,128]{2,1,0:T(8,128)}) custom-call(bf16[256,8,256]{2,1,0:T(8,128)(2,1)} %get-tuple-element.12.fields, bf16[3840,128]{1,0:T(8,128)(2,1)} %get-tuple-element.13.res_h), custom_call_target="tpu_custom_call" | custom-call | tf_op jit(solution)/shard_map/pallas_call | solution.py:739

commit v4 on v3

--- a/solution.py
+++ b/solution.py
@@ -656,16 +656,15 @@
     def put_out(where, v):
         put_relaid(where, fc[0:C, where].astype(F32) + v)
 
+    def put_feat(where, v):
+        put_relaid(where, fc[C:2 * C, where].astype(F32) + v)
+
+    middle(0)
     conv(wo, x3m, put_out)
     put_field(0)
-    middle(0)
     middle(1)
+    gather(0)
     build(x3g, gin, hr.at[GIN], wait_fine(GIN, hr.at[GIN]))
-
-    def put_feat(where, v):
-        put_relaid(where, fc[C:2 * C, where].astype(F32) + v)
-
-    gather(0)
     conv(wt_in, x3g, put_feat)
     put_field(C)
     gather(1)

time: 110 us -> 110 us (level)
  no operation moved by 1% of the time
where the time goes in v4:
time: 110 us
  Pallas kernels  109 us (99%)
    pallas_call x1, Pallas kernels, local(): pl.pallas_call(kernel, out_shape=(jax.ShapeDtypeStruct((2 * C, H, W), BF1...  106 us
    pallas_call x1, Pallas kernels, local(): pl.pallas_call(results, out_shape=(jax.ShapeDtypeStruct((C, H, W), BF16),...  3.13 us

profile of v4, /device:TPU:1, one launch (start us, length us, event | category | flops | bytes accessed | tf_op | source)
XLA Modules:
  0.0 109.7 jit_solution(10528117084833980106)
XLA Ops:
  0.6 105.7 %shard_map.164 = (bf16[256,8,256]{2,1,0:T(8,128)(2,1)}, bf16[3840,128]{1,0:T(8,128)(2,1)}) custom-call(bf16[128,8,256]{2,1,0:T(8,128)(2,1)} %feat.1, bf16[128,8,256]{2,1,0:T(8,128)(2,1)} %cot.1, bf16[1,16,40,256]{3,2,1,0:T(8,128)(2,1)} %blocks.1, s32[1,8,8,8]{3,2,1,0:T(8,128)} %table.1, s32[2,8,256]{2,1,0:T(8,128)} %src.1, f32[2,8,256]{2,1,0:T(8,128)} %wt.1, ...), custom_call_target="tpu_custom_call" | custom-call | tf_op jit(solution)/shard_map/pallas_call | solution.py:725
  106.4 3.1 %shard_map.165 = (bf16[128,8,256]{2,1,0:T(8,128)(2,1)}, bf16[128,8,256]{2,1,0:T(8,128)(2,1)}, f32[9,168,128]{2,1,0:T(8,128)}, f32[9,128,128]{2,1,0:T(8,128)}, f32[9,128,128]{2,1,0:T(8,128)}) custom-call(bf16[256,8,256]{2,1,0:T(8,128)(2,1)} %get-tuple-element.12.fields, bf16[3840,128]{1,0:T(8,128)(2,1)} %get-tuple-element.13.res_h), custom_call_target="tpu_custom_call" | custom-call | tf_op jit(solution)/shard_map/pallas_call | solution.py:738

commit v5 on v3

--- a/solution.py
+++ b/solution.py
@@ -269,7 +269,7 @@
             x3[C:2 * C, r * W:(r + 1) * W] = v
             x3[2 * C:3 * C, r * W:(r + 1) * W] = after.astype(BF16)
 
-    STEP = 512
+    STEP = 1024
 
     def conv(weights, x3, use):
         def body(j, _):
@@ -409,7 +409,7 @@
         act[:, where] = (affine * sigmoid(affine)).astype(BF16)
         return 0
 
-    lax.fori_loop(0, H, activate, 0)
+    lax.fori_loop(0, H, activate, 0, unroll=True)
 
     def send_coarse(f, rows, near, mine, packs):
         half = rows.shape[0] // 2
@@ -533,7 +533,7 @@
         en = e * normed
         return s + e[:, 0:128] + e[:, 128:256], q + en[:, 0:128] + en[:, 128:256]
 
-    s, q = lax.fori_loop(0, H, slopes, (jnp.zeros((C, 128), F32), jnp.zeros((C, 128), F32)))
+    s, q = lax.fori_loop(0, H, slopes, (jnp.zeros((C, 128), F32), jnp.zeros((C, 128), F32)), unroll=True)
 
     jobs = {
         0: (ROWS_OM, s_om, core_om, half_om, r1_om, r2_om, full_om),
@@ -626,7 +626,7 @@
         gin[:, where] = ((slope[:, where] - mean_e - normed * mean_en) * inv_in).astype(BF16)
         return 0
 
-    lax.fori_loop(0, H, finish_in, 0)
+    lax.fori_loop(0, H, finish_in, 0, unroll=True)
 
     taps = C + CC
     for a in range(3):

time: 110 us -> 108 us (0.982)
  Pallas kernels: 109 us -> 107 us
    pallas_call x1, Pallas kernels: 106 us -> 104 us  [local(): pl.pallas_call(kernel, out_shape=(jax.ShapeDtypeStruct((2 * C, H, W), BF1...]
where the time goes in v5:
time: 108 us
  Pallas kernels  107 us (99%)
    pallas_call x1, Pallas kernels, local(): pl.pallas_call(kernel, out_shape=(jax.ShapeDtypeStruct((2 * C, H, W), BF1...  104 us
    pallas_call x1, Pallas kernels, local(): pl.pallas_call(results, out_shape=(jax.ShapeDtypeStruct((C, H, W), BF16),...  3.13 us

profile of v5, /device:TPU:1, one launch (start us, length us, event | category | flops | bytes accessed | tf_op | source)
XLA Modules:
  0.0 108.3 jit_solution(8480645654415876278)
XLA Ops:
  0.6 104.3 %shard_map.164 = (bf16[256,8,256]{2,1,0:T(8,128)(2,1)}, bf16[3840,128]{1,0:T(8,128)(2,1)}) custom-call(bf16[128,8,256]{2,1,0:T(8,128)(2,1)} %feat.1, bf16[128,8,256]{2,1,0:T(8,128)(2,1)} %cot.1, bf16[1,16,40,256]{3,2,1,0:T(8,128)(2,1)} %blocks.1, s32[1,8,8,8]{3,2,1,0:T(8,128)} %table.1, s32[2,8,256]{2,1,0:T(8,128)} %src.1, f32[2,8,256]{2,1,0:T(8,128)} %wt.1, ...), custom_call_target="tpu_custom_call" | custom-call | tf_op jit(solution)/shard_map/pallas_call | solution.py:726
  105.0 3.1 %shard_map.165 = (bf16[128,8,256]{2,1,0:T(8,128)(2,1)}, bf16[128,8,256]{2,1,0:T(8,128)(2,1)}, f32[9,168,128]{2,1,0:T(8,128)}, f32[9,128,128]{2,1,0:T(8,128)}, f32[9,128,128]{2,1,0:T(8,128)}) custom-call(bf16[256,8,256]{2,1,0:T(8,128)(2,1)} %get-tuple-element.12.fields, bf16[3840,128]{1,0:T(8,128)(2,1)} %get-tuple-element.13.res_h), custom_call_target="tpu_custom_call" | custom-call | tf_op jit(solution)/shard_map/pallas_call | solution.py:739
